TPU v7x, 128 devices: a whole 4x4x4 slice. The times are simulated.
128 devices in a mesh: row: 8 (over z, core), col: 8 (over x_lo, y), depth: 2 (over x_hi).
Axes of the slice: x: 4 (x_hi: 2, x_lo: 2; x = x_hi * 2 + x_lo), y: 4, z: 4, core: 2. Of those that a mesh axis runs over, the one named last changes fastest.
Arguments:
- blocks: bfloat16 [256, 16, 4096], P('row', ('col', 'depth')), may hold values from -1 to 1
- pattern: int32 [256, 16], P('row', ('col', 'depth')), may hold values from 0 to 255, as said below
Outputs:
- purified: float32 [2048, 16384], P('row', ('col', 'depth'))
Inputs may be any that keep to these rules, and one draw needn't show every extreme that they name: `pattern`: in every block row, entries j * 1 to j + 1 - 1 name 1 different block columns of j * 16 to j * 16 + 15, in increasing order.
All inputs are finite; a program needn't handle non-finite values.
Results may differ from a plain program's by a relative error of at most 0.0028.
Values may be sent and summed in bfloat16 or wider, within the bound.
No kernel may reach another device: no remote copies, remote signals or barrier semaphores. Data moves between devices by JAX's collectives and lax.ppermute only.
A program may use at most 256 MiB of HBM per device.

v0:
```python
import jax
import jax.numpy as jnp
from jax import lax
from jax.sharding import PartitionSpec as P

BLOCK = 64
KB = 1
SR = 4


def spread(block, axis, owner):
    block = jnp.where(lax.axis_index(axis) == owner, block, jnp.zeros_like(block))
    return lax.psum(block, axis)


def densify(tiles_flat, block_ids, group_width):
    rows, slots = block_ids.shape
    groups = slots // KB
    local_ids = (block_ids % group_width).reshape(rows, groups, KB)
    onehot = (local_ids[..., None] == jnp.arange(group_width, dtype=jnp.int32)).astype(jnp.bfloat16)
    tile_grid = tiles_flat.reshape(rows, groups, KB, BLOCK, BLOCK)
    dense_tiles = jnp.einsum(
        "rgkyz,rgkc->rygcz", tile_grid, onehot, preferred_element_type=jnp.bfloat16
    )
    return dense_tiles.reshape(rows * BLOCK, groups * group_width * BLOCK)


def slab_square(slab_tiles, slab_ids, panel_dense):
    slab_rows, slots = slab_ids.shape
    width = panel_dense.shape[1]
    panel_blocks = panel_dense.reshape(-1, BLOCK, width)
    picked = panel_blocks[slab_ids]
    tile_grid = slab_tiles.reshape(slab_rows, slots, BLOCK, BLOCK)
    result = jnp.einsum("rsyz,rszc->ryc", tile_grid, picked, preferred_element_type=jnp.float32)
    return result.reshape(slab_rows * BLOCK, width)


def body(blocks, pattern):
    row_count = blocks.shape[0]
    group_width = (
        row_count * lax.axis_size("row") // (lax.axis_size("col") * lax.axis_size("depth"))
    )
    column_tiles, column_ids = (
        lax.all_gather(blocks, "row", axis=0, tiled=True),
        lax.all_gather(pattern, "row", axis=0, tiled=True),
    )
    panel_dense = densify(column_tiles, column_ids, group_width)
    row_tiles, row_ids = (
        lax.all_gather(blocks, ("col", "depth"), axis=1, tiled=True),
        lax.all_gather(pattern, ("col", "depth"), axis=1, tiled=True),
    )
    square32 = slab_square(row_tiles[:SR], row_ids[:SR], panel_dense)
    square = square32.astype(jnp.bfloat16)
    first_row = lax.axis_index(("col", "depth")) * group_width
    owner = first_row // row_count
    offset = first_row % row_count
    own_tiles = lax.dynamic_slice_in_dim(row_tiles, offset, group_width, 0)
    own_ids = lax.dynamic_slice_in_dim(row_ids, offset, group_width, 0)
    group_tiles, group_ids = (spread(own_tiles, "row", owner), spread(own_ids, "row", owner))
    group_dense = densify(group_tiles, group_ids, group_width)
    partial_value = jnp.dot(square, group_dense, preferred_element_type=jnp.float32)
    cube_sum = lax.psum_scatter(partial_value, ("col", "depth"), scatter_dimension=1, tiled=True)
    return 3.0 * square32 - 2.0 * cube_sum


def solution(mesh):
    in_specs = (P("row", ("col", "depth"), None), P("row", ("col", "depth")))
    out_specs = P("row", ("col", "depth"))
    return jax.shard_map(body, mesh=mesh, in_specs=in_specs, out_specs=out_specs, check_vma=False)
```

profile of v0, /device:TPU:0, one launch (start us, length us, event | category | flops | bytes accessed | tf_op | source)
XLA Modules:
  0.0 720.2 jit_solution(11672589581873715403)
XLA Ops:
  6.5 0.0 all-gather.4.cloned.1.call-start
  6.5 0.7 all-gather.4.cloned.1.call-update
  7.3 0.0 all-gather.6.cloned.1.call-start
  7.3 0.7 all-gather.6.cloned.1.call-update
  8.0 0.0 all-reduce.4.cloned.1.call-start
  8.1 39.6 %all-gather = s32[16,1,32]{2,1,0:T(1,128)S(1)} all-gather(s32[1,1,32]{2,1,0:T(1,128)} %bitcast.47), channel_id=1, replica_groups=mesh['row'=8,'col'=8,'depth'=2] {'col','depth'}, dimensions={0}, use_global_device_ids=true | all-gather | bytes 2176 | tf_op jit(solution)/shard_map/all_gather | solution.py:50
  47.7 0.1 copy.20
  47.8 0.1 reshape.50
  47.9 1.2 dynamic-slice
  49.8 0.1 broadcast_select_fusion
  49.9 0.8 bitcast_dynamic-update-slice_fusion
  50.6 10.7 %all-reduce.1 = (s32[256]{0:T(256)S(1)}, s32[16,16]{0,1:T(8,128)S(1)}) all-reduce(s32[256]{0:T(256)S(1)} %bitcast_dynamic-update-slice_fusion, s32[16,16]{0,1:T(8,128)S(1)} %bitcast.44), channel_id=1, replica_groups=mesh['row'=8,'col'=8,'depth'=2] {'row'}, use_global_device_ids=true, to_apply=%add | all-reduce | flops 512 | bytes 4096
  61.4 0.1 copy.23
  61.5 0.1 fusion
  61.6 0.0 all-gather.4.cloned.1.call-done
  61.6 4.1 copy.19
  65.7 95.0 %all-gather.6.cloned.1.call-done = bf16[32,16,4096]{2,0,1:T(8,128)(2,1)} async-done(((bf16[32,1,4096]{2,0,1:T(8,128)(2,1)}), bf16[32,16,4096]{2,0,1:T(8,128)(2,1)}) %all-gather.6.cloned.1.call-update) | async-done | bytes 4194320 | tf_op jit(solution)/shard_map/all_gather | solution.py:49
  160.7 2.0 dynamic-slice_select_fusion
  162.7 5.6 reshape.46
  168.3 0.0 all-reduce.4.cloned.1.call-update
  168.3 0.0 reduce-scatter.2.cloned.1.call-start
  168.4 12.7 %broadcast_multiply_fusion = bf16[256,16,64,64]{0,3,1,2:T(8,128)(2,1)} fusion(bf16[256,64,64]{0,2,1:T(8,128)(2,1)} %bitcast.41, bf16[256,16]{0,1:T(8,128)(2,1)S(1)} %fusion.1), kind=kLoop, calls=%fused_computation.2 | loop fusion | flops 16777216 | bytes 35659776 | tf_op jit(solution)/shard_map/rgkyz,rgkc->rygcz/dot_general | solution.py:22
  181.1 46.2 %copy.21 = bf16[256,64,1024]{2,1,0:T(8,128)(2,1)} copy(bf16[256,64,1024]{0,2,1:T(8,128)(2,1)} %bitcast.39) | data formatting | bytes 67108864 | tf_op jit(solution)/shard_map/reshape;reshape | solution.py:31
  227.3 7.4 %gather_fusion = bf16[64,64,1024]{2,1,0:T(8,128)(2,1)} fusion(bf16[256,64,1024]{2,1,0:T(8,128)(2,1)} %copy.21, s32[1024]{0:T(1024)S(1)} %pad_clamp_fusion), kind=kCustom, calls=%fused_computation | custom fusion | bytes 16777472 | tf_op jit(solution)/shard_map/gather | solution.py:32
  234.6 1.4 slice.10
  236.1 0.3 copy.22
  236.4 1.1 reshape.45
  237.5 5.0 fusion.4
  242.5 0.0 all-reduce.4.cloned.1.call-done
  242.6 5.7 copy.24
  248.3 21.1 %multiply_bitcast_fusion = bf16[16,64,16,16,64]{4,3,2,1,0:T(8,128)(2,1)} fusion(bf16[16,16,64,64]{3,1,2,0:T(8,128)(2,1)S(1)} %copy.24, bf16[16,16,16]{2,1,0:T(8,128)(2,1)S(1)} %fusion), kind=kLoop, calls=%fused_computation.1 | loop fusion | flops 16777216 | bytes 35659776 | tf_op jit(solution)/shard_map/rgkyz,rgkc->rygcz/transpose | solution.py:22
  269.4 75.4 %reshape.47 = bf16[1024,16384]{1,0:T(8,128)(2,1)} reshape(bf16[16,64,16,16,64]{4,3,2,1,0:T(8,128)(2,1)} %multiply_bitcast_fusion) | data formatting | bytes 67108864 | tf_op jit(solution)/shard_map/reshape | solution.py:25
  344.8 18.3 %fusion.5 = f32[256,16384]{1,0:T(8,128)} fusion(bf16[256,1024]{1,0:T(8,128)(2,1)S(1)} %bitcast.42, bf16[1024,16384]{1,0:T(8,128)(2,1)} %reshape.47), kind=kOutput, calls=%fused_computation.24 | convolution fusion | flops 8589934592 | bytes 50855936 | tf_op jit(solution)/shard_map/dot_general | solution.py:61
  363.1 0.0 reduce-scatter.2.cloned.1.call-update
  363.1 348.1 %reduce-scatter.2.cloned.1.call-done = f32[256,1024]{1,0:T(8,128)} async-done(((f32[256,16384]{1,0:T(8,128)}), f32[256,1024]{1,0:T(8,128)}) %reduce-scatter.2.cloned.1.call-update) | async-done | bytes 1048592 | tf_op jit(solution)/shard_map/reduce_scatter | solution.py:62
  711.2 2.4 bitcast_subtract_fusion
  (6 shorter events, 0.0 us)
Async XLA Ops:
  6.5 55.1 %all-gather.4.cloned.1.call-start = ((), (), s32[]{:S(2)}) async-start(), calls=%async_computation.1 | async-start | bytes 2359296 | tf_op jit(solution)/shard_map/all_gather | solution.py:44
  7.3 153.5 %all-gather.6.cloned.1.call-start = ((), (), s32[]{:S(2)}) async-start(), calls=%async_computation.2 | async-start | bytes 4456448 | tf_op jit(solution)/shard_map/all_gather | solution.py:49
  8.0 234.5 %all-reduce.4.cloned.1.call-start = ((), (), s32[]{:S(2)}) async-start(), calls=%async_computation.3 | async-start | bytes 8388608 | tf_op jit(solution)/shard_map/psum | solution.py:13
  168.3 542.9 %reduce-scatter.2.cloned.1.call-start = ((), (), s32[]{:S(2)}) async-start(), calls=%async_computation.4 | async-start | bytes 17825792 | tf_op jit(solution)/shard_map/reduce_scatter | solution.py:62
Sparse Core Ops, SparseCore 0:
  9.1 27.8 all-gather.3
  38.6 122.0 all-gather.5
  168.4 68.7 all-reduce.3
  363.2 347.9 reduce-scatter.1
where the time goes:
time: 724 us; the launch traced here: 720 us
  waiting for transfers between devices  445 us (61%)
  local copies, waits for them, and re-layouts  149 us (21%)
  blocking collectives  50.4 us (7%)
  other arithmetic  38.5 us (5%)
  matrix products  23.3 us (3%)
  between operations  13.9 us (2%)
    reduce_scatter x1, waiting for transfers between devices, body(): lax.psum_scatter(partial_value, ('col', 'depth'), scatter_dimension=1, ti...  348 us
    all_gather x1, waiting for transfers between devices, body(): lax.all_gather(blocks, ('col', 'depth'), axis=1, tiled=True)  95 us
    reshape x1, local copies, waits for them, and re-layouts, densify(): return dense_tiles.reshape(rows * BLOCK, groups * group_width * BLOCK)  75.4 us
    another operation x1, local copies, waits for them, and re-layouts, slab_square(): panel_blocks = panel_dense.reshape(-1, BLOCK, width)  46.2 us
    all_gather x1, blocking collectives, body(): lax.all_gather(pattern, ('col', 'depth'), axis=1, tiled=True)  39.6 us
    transpose x1, other arithmetic, densify(): jnp.einsum('rgkyz,rgkc->rygcz', tile_grid, onehot, preferred_element_type...  21.1 us
    dot_general x1, matrix products, body(): jnp.dot(square, group_dense, preferred_element_type=jnp.float32)  18.3 us
  transfers between devices with their start and end apart: 4, of which 2 were waited for; matrix products, arithmetic and copies ran while one was open for 11% of the time, Pallas kernels for 0%

commit v1 on v0

v1 whole, which is shorter than its diff:
```python
import functools

import jax
import jax.numpy as jnp
from jax import lax
from jax.experimental import pallas as pl
from jax.experimental.pallas import tpu as pltpu
from jax.sharding import PartitionSpec as P

AXES = ("row", "col", "depth")
F32, BF16, I32 = jnp.float32, jnp.bfloat16, jnp.int32
PACKED = 1040
SLABP = 144
VMEM_LIMIT = 40 << 20
PARAMS = pltpu.CompilerParams(vmem_limit_bytes=VMEM_LIMIT)


def place(i):
    row, col, depth = i // 16, i // 2 % 8, i % 2
    return row // 2, row % 2, depth * 2 + col // 4, col % 4


def index(z, core, x, y):
    return (z * 2 + core) * 16 + (x % 2 * 4 + y) * 2 + x // 2


def permute(value, target):
    pairs = [(i, index(*target(*place(i)))) for i in range(128)]
    return lax.ppermute(value, AXES, pairs)


def shift(value, z=0, core=0, x=0, y=0):
    return permute(
        value, lambda a, b, c, d: ((a + z) % 4, (b + core) % 2, (c + x) % 4, (d + y) % 4)
    )


def swap_rows_and_y(value):
    def target(z, core, x, y):
        t = z % 2 * 2 + core
        return z // 2 * 2 + y // 2, y % 2, x, t

    return permute(value, target)


def over_row(value):
    ring = [value] + [shift(value, z=d) for d in (1, 3, 2)]
    return ring + [shift(v, core=1) for v in ring]


def pack_kernel(x_ref, pat_ref, packed_ref, slab_ref, rows, nat, turned, ints):
    for e in range(32):
        rows[pl.ds(e, 32, stride=32), :] = x_ref[:, e * 128 : e * 128 + 128].astype(F32)
    for quad in range(8):
        at = pl.ds(quad * 128, 128)
        packed_ref[at, :] = jnp.transpose(rows[at, :]).astype(BF16)
    ints[...] = jnp.zeros_like(ints)
    ints[0:1, 0:32] = pat_ref[...]
    columns = ints[...].astype(F32).astype(BF16)
    packed_ref[1024:1040, :] = columns
    for i in range(4):
        part = rows[i * 32 : i * 32 + 32, :]
        nat[pl.ds(i * 64, 32, stride=2), :] = part
        nat[pl.ds(i * 64 + 1, 32, stride=2), :] = pltpu.roll(part, 64, 1)
    for h in range(2):
        turned[...] = jnp.transpose(nat[h * 128 : h * 128 + 128, :])
        for p in range(2):
            piece = turned[pl.ds(p, 32, stride=2), :].astype(BF16)
            at = h * 64 + p * 32
            for s in range(16):
                slab_ref[s, at : at + 32, :] = piece
    for s in range(16):
        slab_ref[s, 128:144, :] = columns


def pack(blocks, pattern):
    return pl.pallas_call(
        pack_kernel,
        out_shape=(
            jax.ShapeDtypeStruct((PACKED, 128), BF16),
            jax.ShapeDtypeStruct((16, SLABP, 128), BF16),
        ),
        scratch_shapes=[
            pltpu.VMEM((1024, 128), F32),
            pltpu.VMEM((256, 128), F32),
            pltpu.VMEM((128, 128), F32),
            pltpu.VMEM((16, 128), I32),
        ],
        compiler_params=PARAMS,
        name="pack",
    )(blocks, pattern)


def fetch_rows(place_ref, parts, panel, sem):
    z, core = place_ref[0], place_ref[1]
    copies = []
    for n, part in enumerate(parts):
        source_z = lax.rem(z + 4 - (0, 1, 3, 2)[n % 4], 4)
        source_core = core if n < 4 else 1 - core
        copies.append(
            pltpu.make_async_copy(part, panel.at[source_z * 2 + source_core], sem.at[n])
        )
    for copy in copies:
        copy.start()
    return copies


def lane_masks():
    lane = lax.broadcasted_iota(I32, (1, 256), 1)
    return lax.rem(lax.div(lane, 32), 4)


def square_kernel(place_ref, *refs):
    parts, (slab, out32, out16, panel, ints, scal, sem, sem_s) = refs[:8], refs[8:]
    copies = fetch_rows(place_ref, parts, panel, sem)
    out32[...] = jnp.zeros_like(out32)
    for s in range(16):
        ints[8 + s : 9 + s, :] = slab[s, 128:144, :].astype(F32)[0:1, :].astype(I32)
    for copy in copies:
        copy.wait()
    for r in range(8):
        ints[r : r + 1, :] = panel[r, 1024:1040, :].astype(F32)[0:1, :].astype(I32)
    to_scal = pltpu.make_async_copy(ints, scal, sem_s)
    to_scal.start()
    to_scal.wait()
    quarter = lane_masks()
    half = lax.broadcasted_iota(I32, (64, 128), 1) < 64

    def step(s, carry):
        sides = []
        for h in range(2):
            pieces = []
            for p in range(2):
                pieces += [slab[s, h * 64 + p * 32 : h * 64 + p * 32 + 32, :]] * 4
            sides.append(jnp.concatenate(pieces, axis=0))
        rhs = jnp.concatenate(sides, axis=1)
        left, columns = [], []
        for i in range(4):
            c = scal[8 + s, i]
            r, k = lax.div(c, 32), lax.rem(c, 32)
            quad, c4 = lax.div(k, 4), lax.rem(k, 4)
            t = panel[r, pl.ds(pl.multiple_of(quad * 128, 128), 128), :]
            t = jnp.concatenate([t[0:64], t[64:128]], axis=1)
            left.append(t * (quarter == c4).astype(F32).astype(BF16))
            columns.append(lax.rem(scal[r, k], 16))
        out = jnp.dot(jnp.concatenate(left, axis=0), rhs, preferred_element_type=F32)
        for i in range(4):
            h = i // 2
            got = out[i * 64 : i * 64 + 64, h * 128 : h * 128 + 128]
            got = jnp.where(half if i % 2 == 0 else jnp.logical_not(half), got, 0.0)
            out32[h, pl.ds(pl.multiple_of(columns[i] * 64, 64), 64), :] += got
        return carry

    lax.fori_loop(0, 16, step, 0)
    for h in range(2):
        for quad in range(4):
            for p in range(2):
                for c4 in range(4):
                    take = out32[h, pl.ds((quad * 4 + c4) * 64 + p, 32, stride=2), :]
                    at = quad * 256 + p * 128 + c4 * 32
                    out16[h, at : at + 32, :] = take.astype(BF16)


ANY = pl.BlockSpec(memory_space=pl.ANY)
SMEM = pl.BlockSpec(memory_space=pltpu.SMEM)
VMEM = pl.BlockSpec(memory_space=pltpu.VMEM)


def square_of(where, parts, slab):
    return pl.pallas_call(
        square_kernel,
        out_shape=(
            jax.ShapeDtypeStruct((2, 1024, 128), F32),
            jax.ShapeDtypeStruct((2, 1024, 128), BF16),
        ),
        in_specs=[SMEM] + [ANY] * 8 + [VMEM],
        out_specs=(VMEM, VMEM),
        scratch_shapes=[
            pltpu.VMEM((8, PACKED, 128), BF16),
            pltpu.VMEM((24, 128), I32),
            pltpu.SMEM((24, 128), I32),
            pltpu.SemaphoreType.DMA((8,)),
            pltpu.SemaphoreType.DMA,
        ],
        compiler_params=PARAMS,
        name="square",
    )(where, *parts, slab)


def cube_kernel(place_ref, *refs):
    parts, squares = refs[:8], refs[8:12]
    own, out1, out3, out2, panel, sq, acc, ints, scal, sem, sem_q, sem_s = refs[12:]
    x, y = place_ref[2], place_ref[3]
    copies = fetch_rows(place_ref, parts, panel, sem)
    more = []
    for n, part in enumerate(squares):
        source = lax.rem(x + 4 - (0, 1, 3, 2)[n], 4)
        more.append(pltpu.make_async_copy(part, sq.at[source], sem_q.at[n]))
    for copy in more:
        copy.start()
    acc[...] = jnp.zeros_like(acc)
    for copy in copies:
        copy.wait()
    for r in range(8):
        ints[r : r + 1, :] = panel[r, 1024:1040, :].astype(F32)[0:1, :].astype(I32)
    to_scal = pltpu.make_async_copy(ints, scal, sem_s)
    to_scal.start()
    to_scal.wait()
    for copy in more:
        copy.wait()
    quarter = lane_masks()
    masks = [(quarter == n).astype(F32).astype(BF16) for n in range(4)]

    def step(n, carry):
        q, hi, quad = lax.div(n, 8), lax.rem(lax.div(n, 4), 2), lax.rem(n, 4)
        at = pl.ds(pl.multiple_of(quad * 256, 256), 256)
        right = jnp.concatenate([sq[q + 2 * hi, h, at, :] for h in range(2)], axis=1)
        rows = pl.ds(pl.multiple_of((hi * 4 + quad) * 128, 128), 128)
        for there in range(4):
            t = panel[4 * q + there, rows, :]
            t = jnp.concatenate([t[0:64], t[64:128]], axis=1)
            left = jnp.concatenate([t * mask for mask in masks], axis=0)
            out = jnp.dot(left, right, preferred_element_type=F32)
            for c4 in range(4):
                j = lax.rem(scal[4 * q + there, hi * 16 + quad * 4 + c4], 16)
                into = pl.ds(pl.multiple_of(j * 64, 64), 64)
                acc[there, into, :] += out[c4 * 64 : c4 * 64 + 64, :]
        return carry

    lax.fori_loop(0, 16, step, 0)
    own[...] = acc[y]
    for d, ref in ((1, out1), (3, out3), (2, out2)):
        ref[...] = acc[lax.rem(y + d, 4)].astype(BF16)


def cube_of(where, parts, squares):
    return pl.pallas_call(
        cube_kernel,
        out_shape=(
            jax.ShapeDtypeStruct((1024, 256), F32),
            *[jax.ShapeDtypeStruct((1024, 256), BF16)] * 3,
        ),
        in_specs=[SMEM] + [ANY] * 12,
        out_specs=(VMEM,) * 4,
        scratch_shapes=[
            pltpu.VMEM((8, PACKED, 128), BF16),
            pltpu.VMEM((4, 2, 1024, 128), BF16),
            pltpu.VMEM((4, 1024, 256), F32),
            pltpu.VMEM((8, 128), I32),
            pltpu.SMEM((8, 128), I32),
            pltpu.SemaphoreType.DMA((8,)),
            pltpu.SemaphoreType.DMA((4,)),
            pltpu.SemaphoreType.DMA,
        ],
        compiler_params=PARAMS,
        name="cube",
    )(where, *parts, *squares)


def finish_kernel(sq_ref, own_ref, a_ref, b_ref, c_ref, out_ref):
    for m in range(8):
        at = pl.ds(m * 128, 128)
        for h in range(2):
            lanes = pl.ds(h * 128, 128)
            cube = own_ref[at, lanes]
            for ref in (a_ref, b_ref, c_ref):
                cube += ref[at, lanes].astype(F32)
            total = 3.0 * sq_ref[h, at, :] - 2.0 * cube
            out_ref[lanes, at] = jnp.transpose(total)


def finish(square32, own, others):
    return pl.pallas_call(
        finish_kernel,
        out_shape=jax.ShapeDtypeStruct((256, 1024), F32),
        in_specs=[VMEM] * 5,
        out_specs=VMEM,
        compiler_params=PARAMS,
        name="finish",
    )(square32, own, *others)


def body(blocks, pattern):
    row, col, depth = (lax.axis_index(a) for a in AXES)
    where = jnp.stack([row // 2, row % 2, depth * 2 + col // 4, col % 4]).astype(I32)
    packed, slab = pack(blocks.reshape(32, 4096), pattern.reshape(1, 32))
    parts = over_row(packed)
    slab = lax.all_to_all(slab, ("col", "depth"), 0, 0, tiled=True)
    turned = over_row(swap_rows_and_y(packed))
    square32, square16 = square_of(where, parts, slab)
    squares = [square16] + [shift(square16, x=d) for d in (1, 3, 2)]
    own, out1, out3, out2 = cube_of(where, turned, squares)
    others = [shift(out1, y=1), shift(out3, y=3), shift(out2, y=2)]
    return finish(square32, own, others)


def solution(mesh):
    in_specs = (P("row", ("col", "depth"), None), P("row", ("col", "depth")))
    out_specs = P("row", ("col", "depth"))
    return jax.shard_map(body, mesh=mesh, in_specs=in_specs, out_specs=out_specs, check_vma=False)
```

time: 724 us -> 105 us (0.15)
  waiting for transfers between devices: 445 us -> 55.8 us
  local copies, waits for them, and re-layouts: 149 us -> 1.6 us
  blocking collectives: 50.4 us -> 0 us
  other arithmetic: 38.5 us -> 0.08 us
  starting transfers between devices: 0.12 us -> 30.7 us
  matrix products: 23.3 us -> 0 us
  Pallas kernels: 0 us -> 16.4 us
  between operations: 13.9 us -> 0.06 us
    reduce_scatter x1 -> x0, waiting for transfers between devices: 348 us -> none  [body(): lax.psum_scatter(partial_value, ('col', 'depth'), scatter_dimension=1, ti...]
    all_gather x2 -> x0, waiting for transfers between devices: 95 us -> none  [the longest x1 95 us: body(): lax.all_gather(blocks, ('col', 'depth'), axis=1, tiled=True)]
    reshape x2 -> x0, local copies, waits for them, and re-layouts: 76.5 us -> none  [the longest x1 75.4 us: densify(): return dense_tiles.reshape(rows * BLOCK, groups * group_width * BLOCK)]
    ppermute x0 -> x21, waiting for transfers between devices: none -> 55.8 us  [permute(): return lax.ppermute(value, AXES, pairs)]
    another operation x2 -> x0, local copies, waits for them, and re-layouts: 51.8 us -> none  [the longest x1 46.2 us: slab_square(): panel_blocks = panel_dense.reshape(-1, BLOCK, width)]
    all_gather x1 -> x0, blocking collectives: 39.6 us -> none  [body(): lax.all_gather(pattern, ('col', 'depth'), axis=1, tiled=True)]
    ppermute x0 -> x21, starting transfers between devices: none -> 25.8 us  [permute(): return lax.ppermute(value, AXES, pairs)]
    dot_general x2 -> x0, matrix products: 23.3 us -> none  [the longest x1 18.3 us: body(): jnp.dot(square, group_dense, preferred_element_type=jnp.float32)]
  transfers between devices with their start and end apart: 4 -> 22, of which waited for: 2 -> 9; matrix products, arithmetic and copies ran while one was open for 11% -> 0% of each run, Pallas kernels for 0% -> 5%
where the time goes in v1:
time: 105 us
  waiting for transfers between devices  55.8 us (53%)
  starting transfers between devices  30.7 us (29%)
  Pallas kernels  16.4 us (16%)
  local copies, waits for them, and re-layouts  1.6 us (2%)
    ppermute x21, waiting for transfers between devices, permute(): return lax.ppermute(value, AXES, pairs)  55.8 us
    ppermute x21, starting transfers between devices, permute(): return lax.ppermute(value, AXES, pairs)  25.8 us
    pallas_call x1, Pallas kernels, cube_of(): pl.pallas_call(cube_kernel, out_shape=(jax.ShapeDtypeStruct((1024, 256),...  8.02 us
    pallas_call x1, Pallas kernels, square_of(): pl.pallas_call(square_kernel, out_shape=(jax.ShapeDtypeStruct((2, 1024, 1...  5.7 us
    all_to_all x1, starting transfers between devices, body(): slab = lax.all_to_all(slab, ('col', 'depth'), 0, 0, tiled=True)  4.98 us
  transfers between devices with their start and end apart: 22, of which 9 were waited for; matrix products, arithmetic and copies ran while one was open for 0% of the time, Pallas kernels for 5%

profile of v1, /device:TPU:0, one launch (start us, length us, event | category | flops | bytes accessed | tf_op | source)
XLA Modules:
  0.0 104.8 jit_solution(2418578064453170371)
XLA Ops:
  0.0 0.7 copy-done.1
  0.7 0.9 copy-done
  1.6 1.3 %pack.1 = (bf16[1040,128]{1,0:T(8,128)(2,1)S(1)}, bf16[16,144,128]{2,1,0:T(8,128)(2,1)}) custom-call(bf16[32,4096]{1,0:T(8,128)(2,1)S(1)} %bitcast.6, s32[1,32]{1,0:T(1,128)S(1)} %bitcast.7), custom_call_target="tpu_custom_call" | custom-call | tf_op jit(solution)/shard_map/pack/pallas_call | solution.py:77
  3.0 0.7 collective-permute-start.7
  3.6 4.0 %collective-permute-start.2 = (bf16[1040,128]{1,0:T(8,128)(2,1)S(1)}, bf16[1040,128]{1,0:T(8,128)(2,1)S(1)}, u32[]{:S(2)}, u32[]{:S(2)}) collective-permute-start(bf16[1040,128]{1,0:T(8,128)(2,1)S(1)} %get-tuple-element.13.refs_0_), channel_id=1, source_target_pairs={{0,64},{1,65},{2,66},{3,67},{4,68},{5,69},{6,70},{7,71},{8,72},{9,... | collective-permute-start | bytes 798728 | tf_op jit(solution)/shard_map/ppermute | solution.py:29
  7.7 4.7 %collective-permute-start.1 = (bf16[1040,128]{1,0:T(8,128)(2,1)S(1)}, bf16[1040,128]{1,0:T(8,128)(2,1)S(1)}, u32[]{:S(2)}, u32[]{:S(2)}) collective-permute-start(bf16[1040,128]{1,0:T(8,128)(2,1)S(1)} %get-tuple-element.13.refs_0_), channel_id=1, source_target_pairs={{0,96},{1,97},{2,98},{3,99},{4,100},{5,101},{6,102},{7,103},{8,104... | collective-permute-start | bytes 798728 | tf_op jit(solution)/shard_map/ppermute | solution.py:29
  12.4 5.0 %all-to-all-start = ((bf16[16,144,128]{2,1,0:T(8,128)(2,1)}), bf16[16,144,128]{2,1,0:T(8,128)(2,1)S(1)}, u32[]{:S(2)}, u32[]{:S(2)}) async-start(bf16[16,144,128]{2,1,0:T(8,128)(2,1)} %get-tuple-element.14), calls=%async_computation | async-start | bytes 1179648 | tf_op jit(solution)/shard_map/all_to_all | solution.py:288
  17.3 2.1 %collective-permute-start = (bf16[1040,128]{1,0:T(8,128)(2,1)S(1)}, bf16[1040,128]{1,0:T(8,128)(2,1)S(1)}, u32[]{:S(2)}, u32[]{:S(2)}) collective-permute-start(bf16[1040,128]{1,0:T(8,128)(2,1)S(1)} %get-tuple-element.13.refs_0_), channel_id=1, source_target_pairs={{0,32},{1,33},{2,34},{3,35},{4,36},{5,37},{6,38},{7,39},{8,40},{9,... | collective-permute-start | bytes 798728 | tf_op jit(solution)/shard_map/ppermute | solution.py:29
  19.4 0.0 collective-permute-start.3
  19.4 0.0 collective-permute-done.7.refs_0_
  19.4 0.3 collective-permute-start.10
  19.8 0.0 collective-permute-done.2.refs_3_
  19.8 0.7 collective-permute-start.6
  20.4 5.5 %collective-permute-done.1.refs_2_ = bf16[1040,128]{1,0:T(8,128)(2,1)S(1)} collective-permute-done((bf16[1040,128]{1,0:T(8,128)(2,1)S(1)}, bf16[1040,128]{1,0:T(8,128)(2,1)S(1)}, u32[]{:S(2)}, u32[]{:S(2)}) %collective-permute-start.1) | collective-permute-done | bytes 266272 | tf_op jit(solution)/shard_map/ppermute | solution.py:29
  25.9 0.0 collective-permute-start.5
  25.9 6.6 %collective-permute-done.refs_1_ = bf16[1040,128]{1,0:T(8,128)(2,1)S(1)} collective-permute-done((bf16[1040,128]{1,0:T(8,128)(2,1)S(1)}, bf16[1040,128]{1,0:T(8,128)(2,1)S(1)}, u32[]{:S(2)}, u32[]{:S(2)}) %collective-permute-start) | collective-permute-done | bytes 266272 | tf_op jit(solution)/shard_map/ppermute | solution.py:29
  32.5 0.0 collective-permute-start.4
  32.5 0.0 collective-permute-done.3.refs_4_
  32.5 0.5 collective-permute-start.11
  33.0 0.0 collective-permute-done.10.refs_3_
  33.0 0.3 collective-permute-start.9
  33.3 0.0 collective-permute-done.6.refs_7_
  33.3 1.8 %collective-permute-start.8 = (bf16[1040,128]{1,0:T(8,128)(2,1)S(1)}, bf16[1040,128]{1,0:T(8,128)(2,1)}, u32[]{:S(2)}, u32[]{:S(2)}) collective-permute-start(bf16[1040,128]{1,0:T(8,128)(2,1)S(1)} %collective-permute-done.7.refs_0_), channel_id=1, source_target_pairs={{0,32},{1,33},{2,34},{3,35},{4,36},{5,37},{6,38},{7,39},{8,40},{9,... | collective-permute-start | bytes 798728 | tf_op jit(solution)/shard_map/ppermute | solution.py:29
  35.0 0.0 collective-permute-done.5.refs_6_
  35.1 0.0 collective-permute-start.14
  35.1 0.1 pad_add_fusion.place_ref
  35.1 0.0 collective-permute-done.4.refs_5_
  35.1 0.0 all-to-all-done.refs_8_
  35.1 5.7 %square.1 = (f32[2,1024,128]{2,1,0:T(8,128)S(1)}, bf16[2,1024,128]{2,1,0:T(8,128)(2,1)S(1)}) custom-call(s32[4]{0:T(128)S(1)} %pad_add_fusion.place_ref, bf16[1040,128]{1,0:T(8,128)(2,1)S(1)} %get-tuple-element.13.refs_0_, bf16[1040,128]{1,0:T(8,128)(2,1)S(1)} %collective-permute-done.refs_1_, bf16[1040,128]{1,0:T(8,128)(2,1)S(1)} %collective-permute-done.1.refs_2_, ...), custom_call_target="tpu_custom_call" | custom-call | tf_op jit(solution)/shard_map/square/pallas_call | solution.py:170
  40.8 3.1 %collective-permute-start.17 = (bf16[2,1024,128]{2,1,0:T(8,128)(2,1)S(1)}, bf16[2,1024,128]{2,1,0:T(8,128)(2,1)S(1)}, u32[]{:S(2)}, u32[]{:S(2)}) collective-permute-start(bf16[2,1024,128]{2,1,0:T(8,128)(2,1)S(1)} %get-tuple-element.16.refs_8_), channel_id=1, source_target_pairs={{0,1},{1,0},{2,3},{3,2},{4,5},{5,4},{6,7},{7,6},{8,9},{9,8},{10,11... | collective-permute-start | bytes 1572872 | tf_op jit(solution)/shard_map/ppermute | solution.py:29
  44.0 0.0 collective-permute-done.11.refs_4_
  44.0 1.2 %collective-permute-start.16 = (bf16[2,1024,128]{2,1,0:T(8,128)(2,1)S(1)}, bf16[2,1024,128]{2,1,0:T(8,128)(2,1)S(1)}, u32[]{:S(2)}, u32[]{:S(2)}) collective-permute-start(bf16[2,1024,128]{2,1,0:T(8,128)(2,1)S(1)} %get-tuple-element.16.refs_8_), channel_id=1, source_target_pairs={{0,9},{1,8},{2,11},{3,10},{4,13},{5,12},{6,15},{7,14},{8,0},{9,1},... | collective-permute-start | bytes 1572872 | tf_op jit(solution)/shard_map/ppermute | solution.py:29
  45.2 0.8 collective-permute-start.15
  46.0 0.0 collective-permute-start.13
  46.0 0.0 collective-permute-done.14.refs_7_
  46.0 0.5 collective-permute-start.12
  46.5 1.0 collective-permute-done.13.refs_6_
  47.6 0.6 collective-permute-done.12.refs_5_
  48.2 9.0 %collective-permute-done.17.refs_11_ = bf16[2,1024,128]{2,1,0:T(8,128)(2,1)S(1)} collective-permute-done((bf16[2,1024,128]{2,1,0:T(8,128)(2,1)S(1)}, bf16[2,1024,128]{2,1,0:T(8,128)(2,1)S(1)}, u32[]{:S(2)}, u32[]{:S(2)}) %collective-permute-start.17) | collective-permute-done | bytes 524320 | tf_op jit(solution)/shard_map/ppermute | solution.py:29
  57.2 11.0 %collective-permute-done.16.refs_10_ = bf16[2,1024,128]{2,1,0:T(8,128)(2,1)S(1)} collective-permute-done((bf16[2,1024,128]{2,1,0:T(8,128)(2,1)S(1)}, bf16[2,1024,128]{2,1,0:T(8,128)(2,1)S(1)}, u32[]{:S(2)}, u32[]{:S(2)}) %collective-permute-start.16) | collective-permute-done | bytes 524320 | tf_op jit(solution)/shard_map/ppermute | solution.py:29
  68.2 8.0 %cube.1 = (f32[1024,256]{1,0:T(8,128)S(1)}, bf16[1024,256]{1,0:T(8,128)(2,1)S(1)}, bf16[1024,256]{1,0:T(8,128)(2,1)S(1)}, bf16[1024,256]{1,0:T(8,128)(2,1)S(1)}) custom-call(s32[4]{0:T(128)S(1)} %pad_add_fusion.place_ref, bf16[1040,128]{1,0:T(8,128)(2,1)S(1)} %collective-permute-done.7.refs_0_, bf16[1040,128]{1,0:T(8,128)(2,1)} %collective-permute-done.8.refs_1_, ...), custom_call_target="tpu_custom_call" | custom-call | tf_op jit(solution)/shard_map/cube/pallas_call | solution.py:237
  76.2 1.5 %collective-permute-start.18 = (bf16[1024,256]{1,0:T(8,128)(2,1)S(1)}, bf16[1024,256]{1,0:T(8,128)(2,1)S(1)}, u32[]{:S(2)}, u32[]{:S(2)}) collective-permute-start(bf16[1024,256]{1,0:T(8,128)(2,1)S(1)} %get-tuple-element.18), channel_id=1, source_target_pairs={{0,2},{1,3},{2,4},{3,5},{4,6},{5,7},{6,0},{7,1},{8,10},{9,11},{10,... | collective-permute-start | bytes 1572872 | tf_op jit(solution)/shard_map/ppermute | solution.py:29
  77.7 1.8 %collective-permute-start.19 = (bf16[1024,256]{1,0:T(8,128)(2,1)S(1)}, bf16[1024,256]{1,0:T(8,128)(2,1)S(1)}, u32[]{:S(2)}, u32[]{:S(2)}) collective-permute-start(bf16[1024,256]{1,0:T(8,128)(2,1)S(1)} %get-tuple-element.19), channel_id=1, source_target_pairs={{0,6},{1,7},{2,0},{3,1},{4,2},{5,3},{6,4},{7,5},{8,14},{9,15},{10,... | collective-permute-start | bytes 1572872 | tf_op jit(solution)/shard_map/ppermute | solution.py:29
  79.5 1.8 %collective-permute-start.20 = (bf16[1024,256]{1,0:T(8,128)(2,1)S(1)}, bf16[1024,256]{1,0:T(8,128)(2,1)S(1)}, u32[]{:S(2)}, u32[]{:S(2)}) collective-permute-start(bf16[1024,256]{1,0:T(8,128)(2,1)S(1)} %get-tuple-element.20), channel_id=1, source_target_pairs={{0,4},{1,5},{2,6},{3,7},{4,0},{5,1},{6,2},{7,3},{8,12},{9,13},{10,... | collective-permute-start | bytes 1572872 | tf_op jit(solution)/shard_map/ppermute | solution.py:29
  81.3 9.9 %collective-permute-done.18.a_ref = bf16[1024,256]{1,0:T(8,128)(2,1)S(1)} collective-permute-done((bf16[1024,256]{1,0:T(8,128)(2,1)S(1)}, bf16[1024,256]{1,0:T(8,128)(2,1)S(1)}, u32[]{:S(2)}, u32[]{:S(2)}) %collective-permute-start.18) | collective-permute-done | bytes 524320 | tf_op jit(solution)/shard_map/ppermute | solution.py:29
  91.2 1.4 %collective-permute-done.19.b_ref = bf16[1024,256]{1,0:T(8,128)(2,1)S(1)} collective-permute-done((bf16[1024,256]{1,0:T(8,128)(2,1)S(1)}, bf16[1024,256]{1,0:T(8,128)(2,1)S(1)}, u32[]{:S(2)}, u32[]{:S(2)}) %collective-permute-start.19) | collective-permute-done | bytes 524320 | tf_op jit(solution)/shard_map/ppermute | solution.py:29
  92.6 10.8 %collective-permute-done.20.c_ref = bf16[1024,256]{1,0:T(8,128)(2,1)S(1)} collective-permute-done((bf16[1024,256]{1,0:T(8,128)(2,1)S(1)}, bf16[1024,256]{1,0:T(8,128)(2,1)S(1)}, u32[]{:S(2)}, u32[]{:S(2)}) %collective-permute-start.20) | collective-permute-done | bytes 524320 | tf_op jit(solution)/shard_map/ppermute | solution.py:29
  103.4 1.4 %finish.1 = f32[256,1024]{1,0:T(8,128)} custom-call(f32[2,1024,128]{2,1,0:T(8,128)S(1)} %get-tuple-element.15.sq_ref, f32[1024,256]{1,0:T(8,128)S(1)} %get-tuple-element.17.own_ref, bf16[1024,256]{1,0:T(8,128)(2,1)S(1)} %collective-permute-done.18.a_ref, bf16[1024,256]{1,0:T(8,128)(2,1)S(1)} %collective-permute-done.19.b_ref, ...), custom_call_target="tpu_custom_call" | custom-call | tf_op jit(solution)/shard_map/finish/pallas_call | solution.py:273
  (5 shorter events, 0.0 us)
Async XLA Ops:
  0.0 0.7 copy-start.1
  0.7 0.9 copy-start
  3.0 16.5 %collective-permute-start.7 = (bf16[1040,128]{1,0:T(8,128)(2,1)S(1)}, bf16[1040,128]{1,0:T(8,128)(2,1)S(1)}, u32[]{:S(2)}, u32[]{:S(2)}) collective-permute-start(bf16[1040,128]{1,0:T(8,128)(2,1)S(1)} %get-tuple-element.13.refs_0_), channel_id=1, source_target_pairs={{0,0},{1,1},{2,16},{3,17},{4,32},{5,33},{6,48},{7,49},{8,8},{9,9},... | collective-permute-start | bytes 798728 | tf_op jit(solution)/shard_map/ppermute | solution.py:29
  3.6 16.1 %collective-permute-start.2 = (bf16[1040,128]{1,0:T(8,128)(2,1)S(1)}, bf16[1040,128]{1,0:T(8,128)(2,1)S(1)}, u32[]{:S(2)}, u32[]{:S(2)}) collective-permute-start(bf16[1040,128]{1,0:T(8,128)(2,1)S(1)} %get-tuple-element.13.refs_0_), channel_id=1, source_target_pairs={{0,64},{1,65},{2,66},{3,67},{4,68},{5,69},{6,70},{7,71},{8,72},{9,... | collective-permute-start | bytes 798728 | tf_op jit(solution)/shard_map/ppermute | solution.py:29
  7.7 18.2 %collective-permute-start.1 = (bf16[1040,128]{1,0:T(8,128)(2,1)S(1)}, bf16[1040,128]{1,0:T(8,128)(2,1)S(1)}, u32[]{:S(2)}, u32[]{:S(2)}) collective-permute-start(bf16[1040,128]{1,0:T(8,128)(2,1)S(1)} %get-tuple-element.13.refs_0_), channel_id=1, source_target_pairs={{0,96},{1,97},{2,98},{3,99},{4,100},{5,101},{6,102},{7,103},{8,104... | collective-permute-start | bytes 798728 | tf_op jit(solution)/shard_map/ppermute | solution.py:29
  12.4 22.8 %all-to-all-start = ((bf16[16,144,128]{2,1,0:T(8,128)(2,1)}), bf16[16,144,128]{2,1,0:T(8,128)(2,1)S(1)}, u32[]{:S(2)}, u32[]{:S(2)}) async-start(bf16[16,144,128]{2,1,0:T(8,128)(2,1)} %get-tuple-element.14), calls=%async_computation | async-start | bytes 1179648 | tf_op jit(solution)/shard_map/all_to_all | solution.py:288
  17.3 15.2 %collective-permute-start = (bf16[1040,128]{1,0:T(8,128)(2,1)S(1)}, bf16[1040,128]{1,0:T(8,128)(2,1)S(1)}, u32[]{:S(2)}, u32[]{:S(2)}) collective-permute-start(bf16[1040,128]{1,0:T(8,128)(2,1)S(1)} %get-tuple-element.13.refs_0_), channel_id=1, source_target_pairs={{0,32},{1,33},{2,34},{3,35},{4,36},{5,37},{6,38},{7,39},{8,40},{9,... | collective-permute-start | bytes 798728 | tf_op jit(solution)/shard_map/ppermute | solution.py:29
  19.4 13.1 %collective-permute-start.3 = (bf16[1040,128]{1,0:T(8,128)(2,1)S(1)}, bf16[1040,128]{1,0:T(8,128)(2,1)S(1)}, u32[]{:S(2)}, u32[]{:S(2)}) collective-permute-start(bf16[1040,128]{1,0:T(8,128)(2,1)S(1)} %get-tuple-element.13.refs_0_), channel_id=1, source_target_pairs={{0,16},{1,17},{2,18},{3,19},{4,20},{5,21},{6,22},{7,23},{8,24},{9,... | collective-permute-start | bytes 798728 | tf_op jit(solution)/shard_map/ppermute | solution.py:29
  19.4 13.6 %collective-permute-start.10 = (bf16[1040,128]{1,0:T(8,128)(2,1)S(1)}, bf16[1040,128]{1,0:T(8,128)(2,1)S(1)}, u32[]{:S(2)}, u32[]{:S(2)}) collective-permute-start(bf16[1040,128]{1,0:T(8,128)(2,1)S(1)} %collective-permute-done.7.refs_0_), channel_id=1, source_target_pairs={{0,64},{1,65},{2,66},{3,67},{4,68},{5,69},{6,70},{7,71},{8,72},{9,... | collective-permute-start | bytes 798728 | tf_op jit(solution)/shard_map/ppermute | solution.py:29
  19.8 13.5 %collective-permute-start.6 = (bf16[1040,128]{1,0:T(8,128)(2,1)S(1)}, bf16[1040,128]{1,0:T(8,128)(2,1)S(1)}, u32[]{:S(2)}, u32[]{:S(2)}) collective-permute-start(bf16[1040,128]{1,0:T(8,128)(2,1)S(1)} %collective-permute-done.2.refs_3_), channel_id=1, source_target_pairs={{0,16},{1,17},{2,18},{3,19},{4,20},{5,21},{6,22},{7,23},{8,24},{9,... | collective-permute-start | bytes 798728 | tf_op jit(solution)/shard_map/ppermute | solution.py:29
  25.9 9.2 %collective-permute-start.5 = (bf16[1040,128]{1,0:T(8,128)(2,1)S(1)}, bf16[1040,128]{1,0:T(8,128)(2,1)S(1)}, u32[]{:S(2)}, u32[]{:S(2)}) collective-permute-start(bf16[1040,128]{1,0:T(8,128)(2,1)S(1)} %collective-permute-done.1.refs_2_), channel_id=1, source_target_pairs={{0,16},{1,17},{2,18},{3,19},{4,20},{5,21},{6,22},{7,23},{8,24},{9,... | collective-permute-start | bytes 798728 | tf_op jit(solution)/shard_map/ppermute | solution.py:29
  32.5 2.6 %collective-permute-start.4 = (bf16[1040,128]{1,0:T(8,128)(2,1)S(1)}, bf16[1040,128]{1,0:T(8,128)(2,1)}, u32[]{:S(2)}, u32[]{:S(2)}) collective-permute-start(bf16[1040,128]{1,0:T(8,128)(2,1)S(1)} %collective-permute-done.refs_1_), channel_id=1, source_target_pairs={{0,16},{1,17},{2,18},{3,19},{4,20},{5,21},{6,22},{7,23},{8,24},{9,... | collective-permute-start | bytes 798728 | tf_op jit(solution)/shard_map/ppermute | solution.py:29
  32.5 11.5 %collective-permute-start.11 = (bf16[1040,128]{1,0:T(8,128)(2,1)S(1)}, bf16[1040,128]{1,0:T(8,128)(2,1)S(1)}, u32[]{:S(2)}, u32[]{:S(2)}) collective-permute-start(bf16[1040,128]{1,0:T(8,128)(2,1)S(1)} %collective-permute-done.7.refs_0_), channel_id=1, source_target_pairs={{0,16},{1,17},{2,18},{3,19},{4,20},{5,21},{6,22},{7,23},{8,24},{9,... | collective-permute-start | bytes 798728 | tf_op jit(solution)/shard_map/ppermute | solution.py:29
  33.0 12.2 %collective-permute-start.9 = (bf16[1040,128]{1,0:T(8,128)(2,1)S(1)}, bf16[1040,128]{1,0:T(8,128)(2,1)S(1)}, u32[]{:S(2)}, u32[]{:S(2)}) collective-permute-start(bf16[1040,128]{1,0:T(8,128)(2,1)S(1)} %collective-permute-done.7.refs_0_), channel_id=1, source_target_pairs={{0,96},{1,97},{2,98},{3,99},{4,100},{5,101},{6,102},{7,103},{8,104... | collective-permute-start | bytes 798728 | tf_op jit(solution)/shard_map/ppermute | solution.py:29
  33.3 12.7 %collective-permute-start.8 = (bf16[1040,128]{1,0:T(8,128)(2,1)S(1)}, bf16[1040,128]{1,0:T(8,128)(2,1)}, u32[]{:S(2)}, u32[]{:S(2)}) collective-permute-start(bf16[1040,128]{1,0:T(8,128)(2,1)S(1)} %collective-permute-done.7.refs_0_), channel_id=1, source_target_pairs={{0,32},{1,33},{2,34},{3,35},{4,36},{5,37},{6,38},{7,39},{8,40},{9,... | collective-permute-start | bytes 798728 | tf_op jit(solution)/shard_map/ppermute | solution.py:29
  35.1 11.0 %collective-permute-start.14 = (bf16[1040,128]{1,0:T(8,128)(2,1)S(1)}, bf16[1040,128]{1,0:T(8,128)(2,1)}, u32[]{:S(2)}, u32[]{:S(2)}) collective-permute-start(bf16[1040,128]{1,0:T(8,128)(2,1)S(1)} %collective-permute-done.10.refs_3_), channel_id=1, source_target_pairs={{0,16},{1,17},{2,18},{3,19},{4,20},{5,21},{6,22},{7,23},{8,24},{9,... | collective-permute-start | bytes 798728 | tf_op jit(solution)/shard_map/ppermute | solution.py:29
  40.8 16.3 %collective-permute-start.17 = (bf16[2,1024,128]{2,1,0:T(8,128)(2,1)S(1)}, bf16[2,1024,128]{2,1,0:T(8,128)(2,1)S(1)}, u32[]{:S(2)}, u32[]{:S(2)}) collective-permute-start(bf16[2,1024,128]{2,1,0:T(8,128)(2,1)S(1)} %get-tuple-element.16.refs_8_), channel_id=1, source_target_pairs={{0,1},{1,0},{2,3},{3,2},{4,5},{5,4},{6,7},{7,6},{8,9},{9,8},{10,11... | collective-permute-start | bytes 1572872 | tf_op jit(solution)/shard_map/ppermute | solution.py:29
  44.0 24.2 %collective-permute-start.16 = (bf16[2,1024,128]{2,1,0:T(8,128)(2,1)S(1)}, bf16[2,1024,128]{2,1,0:T(8,128)(2,1)S(1)}, u32[]{:S(2)}, u32[]{:S(2)}) collective-permute-start(bf16[2,1024,128]{2,1,0:T(8,128)(2,1)S(1)} %get-tuple-element.16.refs_8_), channel_id=1, source_target_pairs={{0,9},{1,8},{2,11},{3,10},{4,13},{5,12},{6,15},{7,14},{8,0},{9,1},... | collective-permute-start | bytes 1572872 | tf_op jit(solution)/shard_map/ppermute | solution.py:29
  45.2 23.0 %collective-permute-start.15 = (bf16[2,1024,128]{2,1,0:T(8,128)(2,1)S(1)}, bf16[2,1024,128]{2,1,0:T(8,128)(2,1)S(1)}, u32[]{:S(2)}, u32[]{:S(2)}) collective-permute-start(bf16[2,1024,128]{2,1,0:T(8,128)(2,1)S(1)} %get-tuple-element.16.refs_8_), channel_id=1, source_target_pairs={{0,8},{1,9},{2,10},{3,11},{4,12},{5,13},{6,14},{7,15},{8,1},{9,0},... | collective-permute-start | bytes 1572872 | tf_op jit(solution)/shard_map/ppermute | solution.py:29
  46.0 1.5 %collective-permute-start.13 = (bf16[1040,128]{1,0:T(8,128)(2,1)S(1)}, bf16[1040,128]{1,0:T(8,128)(2,1)S(1)}, u32[]{:S(2)}, u32[]{:S(2)}) collective-permute-start(bf16[1040,128]{1,0:T(8,128)(2,1)S(1)} %collective-permute-done.9.refs_2_), channel_id=1, source_target_pairs={{0,16},{1,17},{2,18},{3,19},{4,20},{5,21},{6,22},{7,23},{8,24},{9,... | collective-permute-start | bytes 798728 | tf_op jit(solution)/shard_map/ppermute | solution.py:29
  46.0 2.1 %collective-permute-start.12 = (bf16[1040,128]{1,0:T(8,128)(2,1)}, bf16[1040,128]{1,0:T(8,128)(2,1)S(1)}, u32[]{:S(2)}, u32[]{:S(2)}) collective-permute-start(bf16[1040,128]{1,0:T(8,128)(2,1)} %collective-permute-done.8.refs_1_), channel_id=1, source_target_pairs={{0,16},{1,17},{2,18},{3,19},{4,20},{5,21},{6,22},{7,23},{8,24},{9,... | collective-permute-start | bytes 798728 | tf_op jit(solution)/shard_map/ppermute | solution.py:29
  76.2 15.0 %collective-permute-start.18 = (bf16[1024,256]{1,0:T(8,128)(2,1)S(1)}, bf16[1024,256]{1,0:T(8,128)(2,1)S(1)}, u32[]{:S(2)}, u32[]{:S(2)}) collective-permute-start(bf16[1024,256]{1,0:T(8,128)(2,1)S(1)} %get-tuple-element.18), channel_id=1, source_target_pairs={{0,2},{1,3},{2,4},{3,5},{4,6},{5,7},{6,0},{7,1},{8,10},{9,11},{10,... | collective-permute-start | bytes 1572872 | tf_op jit(solution)/shard_map/ppermute | solution.py:29
  77.7 14.8 %collective-permute-start.19 = (bf16[1024,256]{1,0:T(8,128)(2,1)S(1)}, bf16[1024,256]{1,0:T(8,128)(2,1)S(1)}, u32[]{:S(2)}, u32[]{:S(2)}) collective-permute-start(bf16[1024,256]{1,0:T(8,128)(2,1)S(1)} %get-tuple-element.19), channel_id=1, source_target_pairs={{0,6},{1,7},{2,0},{3,1},{4,2},{5,3},{6,4},{7,5},{8,14},{9,15},{10,... | collective-permute-start | bytes 1572872 | tf_op jit(solution)/shard_map/ppermute | solution.py:29
  79.5 23.9 %collective-permute-start.20 = (bf16[1024,256]{1,0:T(8,128)(2,1)S(1)}, bf16[1024,256]{1,0:T(8,128)(2,1)S(1)}, u32[]{:S(2)}, u32[]{:S(2)}) collective-permute-start(bf16[1024,256]{1,0:T(8,128)(2,1)S(1)} %get-tuple-element.20), channel_id=1, source_target_pairs={{0,4},{1,5},{2,6},{3,7},{4,0},{5,1},{6,2},{7,3},{8,12},{9,13},{10,... | collective-permute-start | bytes 1572872 | tf_op jit(solution)/shard_map/ppermute | solution.py:29

commit v2 on v1

v2 whole, which is shorter than its diff:
```python
import functools

import jax
import jax.numpy as jnp
from jax import lax
from jax.experimental import pallas as pl
from jax.experimental.pallas import tpu as pltpu
from jax.sharding import PartitionSpec as P

AXES = ("row", "col", "depth")
F32, BF16, I32 = jnp.float32, jnp.bfloat16, jnp.int32
HALF = 528
SLABP = 144
VMEM_LIMIT = 40 << 20
PARAMS = pltpu.CompilerParams(vmem_limit_bytes=VMEM_LIMIT)


def place(i):
    row, col, depth = i // 16, i // 2 % 8, i % 2
    return row // 2, row % 2, depth * 2 + col // 4, col % 4


def index(z, core, x, y):
    return (z * 2 + core) * 16 + (x % 2 * 4 + y) * 2 + x // 2


def permute(value, target):
    pairs = [(i, index(*target(*place(i)))) for i in range(128)]
    return lax.ppermute(value, AXES, pairs)


def swap(value, z=0, core=0, x=0, y=0):
    return permute(value, lambda a, b, c, d: (a ^ z, b ^ core, c ^ x, d ^ y))


def after(value, *first):
    return lax.optimization_barrier((value, *first))[0]


def rows_to_y(value):
    def target(z, core, x, y):
        t = z % 2 * 2 + core
        return z // 2 * 2 + y // 2, y % 2, x, t

    return permute(value, target)


FLIPS = (0, 1, 3, 2)


def ring_parts(value):
    return [value] + [swap(value, z=d) for d in FLIPS[1:]]


def fetch_rows(place_ref, ring, other, panel, sem):
    z, core = place_ref[0], place_ref[1]
    copies = []
    for n in range(4):
        row = (z ^ FLIPS[n]) * 2
        mine, others = panel.at[pl.ds((row + core) * 2, 2)], panel.at[pl.ds((row + 1 - core) * 2, 2)]
        copies.append(pltpu.make_async_copy(ring[n], mine, sem.at[n]))
        copies.append(pltpu.make_async_copy(other[n], others, sem.at[4 + n]))
    for copy in copies:
        copy.start()
    return copies


def pack_kernel(x_hbm, pat_hbm, packed_ref, slab_ref, x_ref, pat_ref, rows, nat, turned, ints, sem):
    copies = [
        pltpu.make_async_copy(x_hbm, x_ref, sem.at[0]),
        pltpu.make_async_copy(pat_hbm, pat_ref, sem.at[1]),
    ]
    for copy in copies:
        copy.start()
    for copy in copies:
        copy.wait()
    for e in range(32):
        rows[pl.ds(e, 32, stride=32), :] = x_ref[:, e * 128 : e * 128 + 128].astype(F32)
    ints[...] = jnp.zeros_like(ints)
    for half in range(2):
        for quad in range(4):
            at = pl.ds(half * 512 + quad * 128, 128)
            packed_ref[half, quad * 128 : quad * 128 + 128, :] = jnp.transpose(rows[at, :]).astype(BF16)
        ints[0:1, 0:16] = pat_ref[0:1, half * 16 : half * 16 + 16]
        packed_ref[half, 512:528, :] = ints[...].astype(F32).astype(BF16)
    columns = packed_ref[0, 512:528, :]
    for i in range(4):
        part = rows[i * 32 : i * 32 + 32, :]
        nat[pl.ds(i * 64, 32, stride=2), :] = part
        nat[pl.ds(i * 64 + 1, 32, stride=2), :] = pltpu.roll(part, 64, 1)
    for h in range(2):
        turned[...] = jnp.transpose(nat[h * 128 : h * 128 + 128, :])
        for p in range(2):
            piece = turned[pl.ds(p, 32, stride=2), :].astype(BF16)
            at = h * 64 + p * 32
            for s in range(16):
                slab_ref[s, at : at + 32, :] = piece
    for s in range(16):
        slab_ref[s, 128:144, :] = columns


ANY = pl.BlockSpec(memory_space=pl.ANY)
HBM = pl.BlockSpec(memory_space=pltpu.HBM)
SMEM = pl.BlockSpec(memory_space=pltpu.SMEM)
VMEM = pl.BlockSpec(memory_space=pltpu.VMEM)


def pack(blocks, pattern):
    return pl.pallas_call(
        pack_kernel,
        out_shape=(
            jax.ShapeDtypeStruct((2, HALF, 128), BF16),
            jax.ShapeDtypeStruct((16, SLABP, 128), BF16),
        ),
        in_specs=[HBM, HBM],
        out_specs=(VMEM, VMEM),
        scratch_shapes=[
            pltpu.VMEM((32, 4096), BF16),
            pltpu.VMEM((1, 32), I32),
            pltpu.VMEM((1024, 128), F32),
            pltpu.VMEM((256, 128), F32),
            pltpu.VMEM((128, 128), F32),
            pltpu.VMEM((16, 128), I32),
            pltpu.SemaphoreType.DMA((2,)),
        ],
        compiler_params=pltpu.CompilerParams(vmem_limit_bytes=62 << 20),
        name="pack",
    )(blocks, pattern)


def read_columns(panel, ints):
    for n in range(16):
        row = panel[n, 512:528, :].astype(F32)[0:1, :]
        ints[n : n + 1, :] = row.astype(I32)


def lane_masks():
    lane = lax.broadcasted_iota(I32, (1, 256), 1)
    return lax.rem(lax.div(lane, 32), 4)


def square_kernel(place_ref, *refs):
    ring, other, slab_ref = refs[:4], refs[4:8], refs[8]
    out32, out_a, out_b, panel, slab, ints, scal, sem = refs[9:]
    copies = fetch_rows(place_ref, ring, other, panel, sem)
    fetch_slab = pltpu.make_async_copy(slab_ref, slab, sem.at[8])
    fetch_slab.start()
    out32[...] = jnp.zeros_like(out32)
    fetch_slab.wait()
    for s in range(16):
        ints[16 + s : 17 + s, :] = slab[s, 128:144, :].astype(F32)[0:1, :].astype(I32)
    for copy in copies:
        copy.wait()
    read_columns(panel, ints)
    to_scal = pltpu.make_async_copy(ints, scal, sem.at[0])
    to_scal.start()
    to_scal.wait()
    quarter = lane_masks()
    half = lax.broadcasted_iota(I32, (64, 128), 1) < 64

    def step(s, carry):
        sides = []
        for h in range(2):
            pieces = []
            for p in range(2):
                pieces += [slab[s, h * 64 + p * 32 : h * 64 + p * 32 + 32, :]] * 4
            sides.append(jnp.concatenate(pieces, axis=0))
        rhs = jnp.concatenate(sides, axis=1)
        left, columns = [], []
        for i in range(4):
            c = scal[16 + s, i]
            half_row, k = lax.div(c, 16), lax.rem(c, 16)
            quad, c4 = lax.div(k, 4), lax.rem(k, 4)
            rows = pl.ds(pl.multiple_of(quad * 128, 128), 128)
            t = panel[half_row, rows, :]
            t = jnp.concatenate([t[0:64], t[64:128]], axis=1)
            left.append(t * (quarter == c4).astype(F32).astype(BF16))
            columns.append(lax.rem(scal[half_row, k], 16))
        out = jnp.dot(jnp.concatenate(left, axis=0), rhs, preferred_element_type=F32)
        for i in range(4):
            h = i // 2
            got = out[i * 64 : i * 64 + 64, h * 128 : h * 128 + 128]
            got = jnp.where(half if i % 2 == 0 else jnp.logical_not(half), got, 0.0)
            out32[h, pl.ds(pl.multiple_of(columns[i] * 64, 64), 64), :] += got
        return carry

    lax.fori_loop(0, 16, step, 0, unroll=4)
    for h in range(2):
        for quad in range(4):
            for p in range(2):
                for c4 in range(4):
                    take = out32[h, pl.ds((quad * 4 + c4) * 64 + p, 32, stride=2), :]
                    at = quad * 256 + p * 128 + c4 * 32
                    (out_a, out_b)[h][at : at + 32, :] = take.astype(BF16)


def square_of(where, ring, other, slab):
    return pl.pallas_call(
        square_kernel,
        out_shape=(
            jax.ShapeDtypeStruct((2, 1024, 128), F32),
            *[jax.ShapeDtypeStruct((1024, 128), BF16)] * 2,
        ),
        in_specs=[SMEM] + [ANY] * 9,
        out_specs=(VMEM,) * 3,
        scratch_shapes=[
            pltpu.VMEM((16, HALF, 128), BF16),
            pltpu.VMEM((16, SLABP, 128), BF16),
            pltpu.VMEM((32, 128), I32),
            pltpu.SMEM((32, 128), I32),
            pltpu.SemaphoreType.DMA((9,)),
        ],
        compiler_params=PARAMS,
        name="square",
    )(where, *ring, *other, slab)


def cube_kernel(place_ref, *refs):
    ring, other, squares, outs = refs[:4], refs[4:8], refs[8:12], refs[12:16]
    panel, sq, acc, ints, scal, sem = refs[16:]
    x, y = place_ref[2], place_ref[3]
    copies = fetch_rows(place_ref, ring, other, panel, sem)
    more = []
    for n, part in enumerate(squares):
        more.append(pltpu.make_async_copy(part, sq.at[x ^ FLIPS[n]], sem.at[8 + n]))
    for copy in more:
        copy.start()
    acc[...] = jnp.zeros_like(acc)
    for copy in copies:
        copy.wait()
    read_columns(panel, ints)
    to_scal = pltpu.make_async_copy(ints, scal, sem.at[0])
    to_scal.start()
    to_scal.wait()
    for copy in more:
        copy.wait()
    quarter = lane_masks()
    masks = [(quarter == n).astype(F32).astype(BF16) for n in range(4)]

    def step(n, carry):
        source, quad = lax.div(n, 4), lax.rem(n, 4)
        right = sq[source, pl.ds(pl.multiple_of(quad * 256, 256), 256), :]
        rows = pl.ds(pl.multiple_of(quad * 128, 128), 128)
        for there in range(4):
            half_row = 8 * lax.rem(source, 2) + 2 * there + lax.div(source, 2)
            t = panel[half_row, rows, :]
            t = jnp.concatenate([t[0:64], t[64:128]], axis=1)
            left = jnp.concatenate([t * mask for mask in masks], axis=0)
            out = jnp.dot(left, right, preferred_element_type=F32)
            for c4 in range(4):
                j = lax.rem(scal[half_row, quad * 4 + c4], 16)
                into = pl.ds(pl.multiple_of(j * 64, 64), 64)
                acc[there, into, :] += out[c4 * 64 : c4 * 64 + 64, :]
        return carry

    lax.fori_loop(0, 16, step, 0, unroll=4)
    for n, out in enumerate(outs):
        out[...] = acc[y ^ FLIPS[n]].astype(out.dtype)


def cube_of(where, ring, other, squares):
    return pl.pallas_call(
        cube_kernel,
        out_shape=(
            jax.ShapeDtypeStruct((1024, 128), F32),
            *[jax.ShapeDtypeStruct((1024, 128), BF16)] * 3,
        ),
        in_specs=[SMEM] + [ANY] * 12,
        out_specs=(VMEM,) * 4,
        scratch_shapes=[
            pltpu.VMEM((16, HALF, 128), BF16),
            pltpu.VMEM((4, 1024, 128), BF16),
            pltpu.VMEM((4, 1024, 128), F32),
            pltpu.VMEM((16, 128), I32),
            pltpu.SMEM((16, 128), I32),
            pltpu.SemaphoreType.DMA((12,)),
        ],
        compiler_params=PARAMS,
        name="cube",
    )(where, *ring, *other, *squares)


def finish_kernel(sq_ref, *refs):
    out_ref = refs[8]
    for m in range(8):
        at = pl.ds(m * 128, 128)
        for h in range(2):
            cube = refs[4 * h][at, :]
            for ref in refs[4 * h + 1 : 4 * h + 4]:
                cube += ref[at, :].astype(F32)
            total = 3.0 * sq_ref[h, at, :] - 2.0 * cube
            out_ref[h * 128 : h * 128 + 128, at] = jnp.transpose(total)


def finish(square32, cubes):
    return pl.pallas_call(
        finish_kernel,
        out_shape=jax.ShapeDtypeStruct((256, 1024), F32),
        in_specs=[VMEM] * 9,
        out_specs=VMEM,
        compiler_params=PARAMS,
        name="finish",
    )(square32, *cubes)


def body(blocks, pattern):
    row, col, depth = (lax.axis_index(a) for a in AXES)
    where = jnp.stack([row // 2, row % 2, depth * 2 + col // 4, col % 4]).astype(I32)
    packed, slab = pack(blocks.reshape(32, 4096), pattern.reshape(1, 32))
    ring = ring_parts(packed)
    other = [swap(v, core=1) for v in ring]
    slab = lax.all_to_all(slab, ("col", "depth"), 0, 0, tiled=True)
    turned_ring = ring_parts(rows_to_y(packed))
    turned_other = None
    square32, *squares = square_of(where, ring, other, slab)
    cubes, moved = [], [()] * 3
    for mine in squares:
        moved = [swap(after(mine, *first), x=d) for d, first in zip(FLIPS[1:], moved)]
        if turned_other is None:
            turned_other = [swap(after(v, moved[0]), core=1) for v in turned_ring]
        own, *outs = cube_of(where, turned_ring, turned_other, [mine, *moved])
        moved = [(v,) for v in moved]
        outs = [swap(v, y=d) for v, d in zip(outs, FLIPS[1:])]
        cubes += [own, *outs]
    return finish(square32, cubes)


def solution(mesh):
    in_specs = (P("row", ("col", "depth"), None), P("row", ("col", "depth")))
    out_specs = P("row", ("col", "depth"))
    return jax.shard_map(body, mesh=mesh, in_specs=in_specs, out_specs=out_specs, check_vma=False)
```

time: 105 us -> 92.4 us (0.88)
  waiting for transfers between devices: 55.8 us -> 33.3 us
  starting transfers between devices: 30.7 us -> 41.2 us
  local copies, waits for them, and re-layouts: 1.6 us -> 0.01 us
    ppermute x21 -> x27, waiting for transfers between devices: 55.8 us -> 33.3 us  [permute(): return lax.ppermute(value, AXES, pairs)]
    ppermute x21 -> x27, starting transfers between devices: 25.8 us -> 34 us  [permute(): return lax.ppermute(value, AXES, pairs)]
    pallas_call x2 -> x3, Pallas kernels: 9.37 us -> 11.9 us  [the longest x2 9.61 us: cube_of(): pl.pallas_call(cube_kernel, out_shape=(jax.ShapeDtypeStruct((1024, 128),...]
    all_to_all x1, starting transfers between devices: 4.98 us -> 7.17 us  [body(): slab = lax.all_to_all(slab, ('col', 'depth'), 0, 0, tiled=True)]
    unnamed x4 -> x2, local copies, waits for them, and re-layouts: 1.6 us -> 0.01 us
    pallas_call x1, Pallas kernels: 5.7 us -> 4.14 us  [square_of(): pl.pallas_call(square_kernel, out_shape=(jax.ShapeDtypeStruct((2, 1024, 1...]
  transfers between devices with their start and end apart: 22 -> 28, of which waited for: 9 -> 8; matrix products, arithmetic and copies ran while one was open for 0% -> 0% of each run, Pallas kernels for 5% -> 15%
where the time goes in v2:
time: 92.4 us; the launch traced here: 92.1 us
  starting transfers between devices  41.2 us (45%)
  waiting for transfers between devices  33.3 us (36%)
  Pallas kernels  17.4 us (19%)
    ppermute x27, starting transfers between devices, permute(): return lax.ppermute(value, AXES, pairs)  34 us
    ppermute x27, waiting for transfers between devices, permute(): return lax.ppermute(value, AXES, pairs)  33.3 us
    pallas_call x2, Pallas kernels, cube_of(): pl.pallas_call(cube_kernel, out_shape=(jax.ShapeDtypeStruct((1024, 128),...  9.61 us
    all_to_all x1, starting transfers between devices, body(): slab = lax.all_to_all(slab, ('col', 'depth'), 0, 0, tiled=True)  7.17 us
    pallas_call x1, Pallas kernels, square_of(): pl.pallas_call(square_kernel, out_shape=(jax.ShapeDtypeStruct((2, 1024, 1...  4.14 us
    pallas_call x1, Pallas kernels, pack(): pl.pallas_call(pack_kernel, out_shape=(jax.ShapeDtypeStruct((2, HALF, 128...  2.31 us
  transfers between devices with their start and end apart: 28, of which 8 were waited for; matrix products, arithmetic and copies ran while one was open for 0% of the time, Pallas kernels for 15%

profile of v2, /device:TPU:0, one launch (start us, length us, event | category | flops | bytes accessed | tf_op | source)
XLA Modules:
  0.0 92.1 jit_solution(16463427349516769801)
XLA Ops:
  0.0 2.3 %pack.1 = (bf16[2,528,128]{2,1,0:T(8,128)(2,1)}, bf16[16,144,128]{2,1,0:T(8,128)(2,1)}) custom-call(bf16[32,4096]{1,0:T(8,128)(2,1)} %bitcast.6, s32[1,32]{1,0:T(1,128)} %bitcast.7), custom_call_target="tpu_custom_call" | custom-call | tf_op jit(solution)/shard_map/pack/pallas_call | solution.py:109
  2.3 2.1 %collective-permute-start = (bf16[2,528,128]{2,1,0:T(8,128)(2,1)}, bf16[2,528,128]{2,1,0:T(8,128)(2,1)S(1)}, u32[]{:S(2)}, u32[]{:S(2)}) collective-permute-start(bf16[2,528,128]{2,1,0:T(8,128)(2,1)} %get-tuple-element.25.refs_0_), channel_id=1, source_target_pairs={{0,32},{1,33},{2,34},{3,35},{4,36},{5,37},{6,38},{7,39},{8,40},{9,... | collective-permute-start | bytes 811016 | tf_op jit(solution)/shard_map/ppermute | solution.py:29
  4.4 7.2 %all-to-all-start = ((bf16[16,144,128]{2,1,0:T(8,128)(2,1)}), bf16[16,144,128]{2,1,0:T(8,128)(2,1)S(1)}, u32[]{:S(2)}, u32[]{:S(2)}) async-start(bf16[16,144,128]{2,1,0:T(8,128)(2,1)} %get-tuple-element.26), calls=%async_computation | async-start | bytes 1179648 | tf_op jit(solution)/shard_map/all_to_all | solution.py:312
  11.6 2.6 %collective-permute-start.1 = (bf16[2,528,128]{2,1,0:T(8,128)(2,1)S(1)}, bf16[2,528,128]{2,1,0:T(8,128)(2,1)S(1)}, u32[]{:S(2)}, u32[]{:S(2)}) collective-permute-start(bf16[2,528,128]{2,1,0:T(8,128)(2,1)S(1)} %copy-done), channel_id=1, source_target_pairs={{0,96},{1,97},{2,98},{3,99},{4,100},{5,101},{6,102},{7,103},{8,104... | collective-permute-start | bytes 811016 | tf_op jit(solution)/shard_map/ppermute | solution.py:29
  14.2 1.2 %collective-permute-start.2 = (bf16[2,528,128]{2,1,0:T(8,128)(2,1)S(1)}, bf16[2,528,128]{2,1,0:T(8,128)(2,1)S(1)}, u32[]{:S(2)}, u32[]{:S(2)}) collective-permute-start(bf16[2,528,128]{2,1,0:T(8,128)(2,1)S(1)} %copy-done), channel_id=1, source_target_pairs={{0,64},{1,65},{2,66},{3,67},{4,68},{5,69},{6,70},{7,71},{8,72},{9,... | collective-permute-start | bytes 811016 | tf_op jit(solution)/shard_map/ppermute | solution.py:29
  15.3 0.7 collective-permute-start.7
  16.0 3.3 %collective-permute-start.3 = (bf16[2,528,128]{2,1,0:T(8,128)(2,1)S(1)}, bf16[2,528,128]{2,1,0:T(8,128)(2,1)S(1)}, u32[]{:S(2)}, u32[]{:S(2)}) collective-permute-start(bf16[2,528,128]{2,1,0:T(8,128)(2,1)S(1)} %copy-done), channel_id=1, source_target_pairs={{0,16},{1,17},{2,18},{3,19},{4,20},{5,21},{6,22},{7,23},{8,24},{9,... | collective-permute-start | bytes 811016 | tf_op jit(solution)/shard_map/ppermute | solution.py:29
  19.4 0.0 collective-permute-done.refs_1_
  19.4 0.1 collective-permute-start.4
  19.5 6.9 %collective-permute-done.1.refs_2_ = bf16[2,528,128]{2,1,0:T(8,128)(2,1)S(1)} collective-permute-done((bf16[2,528,128]{2,1,0:T(8,128)(2,1)S(1)}, bf16[2,528,128]{2,1,0:T(8,128)(2,1)S(1)}, u32[]{:S(2)}, u32[]{:S(2)}) %collective-permute-start.1) | collective-permute-done | bytes 270368 | tf_op jit(solution)/shard_map/ppermute | solution.py:29
  26.3 0.0 collective-permute-done.2.refs_3_
  26.3 0.5 collective-permute-start.6
  26.8 0.0 collective-permute-done.7.refs_0_
  26.9 0.6 collective-permute-start.8
  27.4 0.0 collective-permute-done.3.refs_4_
  27.4 2.3 %collective-permute-start.9 = (bf16[2,528,128]{2,1,0:T(8,128)(2,1)S(1)}, bf16[2,528,128]{2,1,0:T(8,128)(2,1)S(1)}, u32[]{:S(2)}, u32[]{:S(2)}) collective-permute-start(bf16[2,528,128]{2,1,0:T(8,128)(2,1)S(1)} %collective-permute-done.7.refs_0_), channel_id=1, source_target_pairs={{0,96},{1,97},{2,98},{3,99},{4,100},{5,101},{6,102},{7,103},{8,104... | collective-permute-start | bytes 811016 | tf_op jit(solution)/shard_map/ppermute | solution.py:29
  29.8 1.2 %collective-permute-start.10 = (bf16[2,528,128]{2,1,0:T(8,128)(2,1)S(1)}, bf16[2,528,128]{2,1,0:T(8,128)(2,1)S(1)}, u32[]{:S(2)}, u32[]{:S(2)}) collective-permute-start(bf16[2,528,128]{2,1,0:T(8,128)(2,1)S(1)} %collective-permute-done.7.refs_0_), channel_id=1, source_target_pairs={{0,64},{1,65},{2,66},{3,67},{4,68},{5,69},{6,70},{7,71},{8,72},{9,... | collective-permute-start | bytes 811016 | tf_op jit(solution)/shard_map/ppermute | solution.py:29
  31.0 0.1 pad_add_fusion.place_ref
  31.1 0.0 collective-permute-done.6.refs_7_
  31.1 0.0 all-to-all-done.refs_8_
  31.1 4.1 %square.1 = (f32[2,1024,128]{2,1,0:T(8,128)S(1)}, bf16[1024,128]{1,0:T(8,128)(2,1)S(1)}, bf16[1024,128]{1,0:T(8,128)(2,1)S(1)}) custom-call(s32[4]{0:T(128)S(1)} %pad_add_fusion.place_ref, bf16[2,528,128]{2,1,0:T(8,128)(2,1)S(1)} %copy-done, bf16[2,528,128]{2,1,0:T(8,128)(2,1)S(1)} %collective-permute-done.refs_1_, ...), custom_call_target="tpu_custom_call" | custom-call | tf_op jit(solution)/shard_map/square/pallas_call | solution.py:198
  35.2 1.7 %collective-permute-start.11 = (bf16[1024,128]{1,0:T(8,128)(2,1)S(1)}, bf16[1024,128]{1,0:T(8,128)(2,1)S(1)}, u32[]{:S(2)}, u32[]{:S(2)}) collective-permute-start(bf16[1024,128]{1,0:T(8,128)(2,1)S(1)} %get-tuple-element.28.refs_8_), channel_id=1, source_target_pairs={{0,8},{1,9},{2,10},{3,11},{4,12},{5,13},{6,14},{7,15},{8,0},{9,1},... | collective-permute-start | bytes 786440 | tf_op jit(solution)/shard_map/ppermute | solution.py:29
  36.9 2.1 %collective-permute-start.16 = (bf16[1024,128]{1,0:T(8,128)(2,1)S(1)}, bf16[1024,128]{1,0:T(8,128)(2,1)S(1)}, u32[]{:S(2)}, u32[]{:S(2)}) collective-permute-start(bf16[1024,128]{1,0:T(8,128)(2,1)S(1)} %get-tuple-element.28.refs_8_), channel_id=1, source_target_pairs={{0,9},{1,8},{2,11},{3,10},{4,13},{5,12},{6,15},{7,14},{8,1},{9,0},... | collective-permute-start | bytes 786440 | tf_op jit(solution)/shard_map/ppermute | solution.py:29
  39.0 5.4 %collective-permute-done.11.refs_9_ = bf16[1024,128]{1,0:T(8,128)(2,1)S(1)} collective-permute-done((bf16[1024,128]{1,0:T(8,128)(2,1)S(1)}, bf16[1024,128]{1,0:T(8,128)(2,1)S(1)}, u32[]{:S(2)}, u32[]{:S(2)}) %collective-permute-start.11) | collective-permute-done | bytes 262176 | tf_op jit(solution)/shard_map/ppermute | solution.py:29
  44.3 0.2 collective-permute-start.12
  44.6 0.3 collective-permute-start.13
  44.9 0.0 collective-permute-done.9.refs_2_
  44.9 0.2 collective-permute-start.14
  45.1 0.3 collective-permute-start.15
  45.4 1.5 %collective-permute-done.16.refs_10_ = bf16[1024,128]{1,0:T(8,128)(2,1)S(1)} collective-permute-done((bf16[1024,128]{1,0:T(8,128)(2,1)S(1)}, bf16[1024,128]{1,0:T(8,128)(2,1)S(1)}, u32[]{:S(2)}, u32[]{:S(2)}) %collective-permute-start.16) | collective-permute-done | bytes 262176 | tf_op jit(solution)/shard_map/ppermute | solution.py:29
  46.8 1.4 %collective-permute-start.17 = (bf16[1024,128]{1,0:T(8,128)(2,1)S(1)}, bf16[1024,128]{1,0:T(8,128)(2,1)S(1)}, u32[]{:S(2)}, u32[]{:S(2)}) collective-permute-start(bf16[1024,128]{1,0:T(8,128)(2,1)S(1)} %get-tuple-element.28.refs_8_), channel_id=1, source_target_pairs={{0,1},{1,0},{2,3},{3,2},{4,5},{5,4},{6,7},{7,6},{8,9},{9,8},{10,11... | collective-permute-start | bytes 786440 | tf_op jit(solution)/shard_map/ppermute | solution.py:29
  48.2 8.1 %collective-permute-done.17.refs_11_ = bf16[1024,128]{1,0:T(8,128)(2,1)S(1)} collective-permute-done((bf16[1024,128]{1,0:T(8,128)(2,1)S(1)}, bf16[1024,128]{1,0:T(8,128)(2,1)S(1)}, u32[]{:S(2)}, u32[]{:S(2)}) %collective-permute-start.17) | collective-permute-done | bytes 262176 | tf_op jit(solution)/shard_map/ppermute | solution.py:29
  56.3 0.5 collective-permute-start.21
  56.8 1.8 %collective-permute-start.22 = (bf16[1024,128]{1,0:T(8,128)(2,1)S(1)}, bf16[1024,128]{1,0:T(8,128)(2,1)S(1)}, u32[]{:S(2)}, u32[]{:S(2)}) collective-permute-start(bf16[1024,128]{1,0:T(8,128)(2,1)S(1)} %get-tuple-element.40.refs_8_), channel_id=1, source_target_pairs={{0,9},{1,8},{2,11},{3,10},{4,13},{5,12},{6,15},{7,14},{8,1},{9,0},... | collective-permute-start | bytes 786440 | tf_op jit(solution)/shard_map/ppermute | solution.py:29
  58.6 1.8 %collective-permute-start.23 = (bf16[1024,128]{1,0:T(8,128)(2,1)S(1)}, bf16[1024,128]{1,0:T(8,128)(2,1)S(1)}, u32[]{:S(2)}, u32[]{:S(2)}) collective-permute-start(bf16[1024,128]{1,0:T(8,128)(2,1)S(1)} %get-tuple-element.40.refs_8_), channel_id=1, source_target_pairs={{0,1},{1,0},{2,3},{3,2},{4,5},{5,4},{6,7},{7,6},{8,9},{9,8},{10,11... | collective-permute-start | bytes 786440 | tf_op jit(solution)/shard_map/ppermute | solution.py:29
  60.4 4.8 %cube.2 = (f32[1024,128]{1,0:T(8,128)S(1)}, bf16[1024,128]{1,0:T(8,128)(2,1)S(1)}, bf16[1024,128]{1,0:T(8,128)(2,1)S(1)}, bf16[1024,128]{1,0:T(8,128)(2,1)S(1)}) custom-call(s32[4]{0:T(128)S(1)} %pad_add_fusion.place_ref, bf16[2,528,128]{2,1,0:T(8,128)(2,1)S(1)} %collective-permute-done.7.refs_0_, bf16[2,528,128]{2,1,0:T(8,128)(2,1)S(1)} %collective-permute-done.8.refs_1_, ...), custom_call_target="tpu_custom_call" | custom-call | tf_op jit(solution)/shard_map/cube/pallas_call | solution.py:262
  65.2 0.1 collective-permute-start.18
  65.3 3.4 %collective-permute-start.19 = (bf16[1024,128]{1,0:T(8,128)(2,1)S(1)}, bf16[1024,128]{1,0:T(8,128)(2,1)S(1)}, u32[]{:S(2)}, u32[]{:S(2)}) collective-permute-start(bf16[1024,128]{1,0:T(8,128)(2,1)S(1)} %get-tuple-element.35), channel_id=1, source_target_pairs={{0,6},{1,7},{2,4},{3,5},{4,2},{5,3},{6,0},{7,1},{8,14},{9,15},{10,... | collective-permute-start | bytes 786440 | tf_op jit(solution)/shard_map/ppermute | solution.py:29
  68.7 0.6 collective-permute-start.20
  69.4 1.4 %collective-permute-done.22.refs_10_ = bf16[1024,128]{1,0:T(8,128)(2,1)S(1)} collective-permute-done((bf16[1024,128]{1,0:T(8,128)(2,1)S(1)}, bf16[1024,128]{1,0:T(8,128)(2,1)S(1)}, u32[]{:S(2)}, u32[]{:S(2)}) %collective-permute-start.22) | collective-permute-done | bytes 262176 | tf_op jit(solution)/shard_map/ppermute | solution.py:29
  70.8 4.8 %cube.3 = (f32[1024,128]{1,0:T(8,128)S(1)}, bf16[1024,128]{1,0:T(8,128)(2,1)S(1)}, bf16[1024,128]{1,0:T(8,128)(2,1)S(1)}, bf16[1024,128]{1,0:T(8,128)(2,1)S(1)}) custom-call(s32[4]{0:T(128)S(1)} %pad_add_fusion.place_ref, bf16[2,528,128]{2,1,0:T(8,128)(2,1)S(1)} %collective-permute-done.7.refs_0_, bf16[2,528,128]{2,1,0:T(8,128)(2,1)S(1)} %collective-permute-done.8.refs_1_, ...), custom_call_target="tpu_custom_call" | custom-call | tf_op jit(solution)/shard_map/cube/pallas_call | solution.py:262
  75.6 0.7 collective-permute-start.24
  76.3 3.7 %collective-permute-start.25 = (bf16[1024,128]{1,0:T(8,128)(2,1)S(1)}, bf16[1024,128]{1,0:T(8,128)(2,1)S(1)}, u32[]{:S(2)}, u32[]{:S(2)}) collective-permute-start(bf16[1024,128]{1,0:T(8,128)(2,1)S(1)} %get-tuple-element.43), channel_id=1, source_target_pairs={{0,6},{1,7},{2,4},{3,5},{4,2},{5,3},{6,0},{7,1},{8,14},{9,15},{10,... | collective-permute-start | bytes 786440 | tf_op jit(solution)/shard_map/ppermute | solution.py:29
  80.0 0.6 collective-permute-start.26
  80.6 4.4 %collective-permute-done.24.refs_5_ = bf16[1024,128]{1,0:T(8,128)(2,1)S(1)} collective-permute-done((bf16[1024,128]{1,0:T(8,128)(2,1)S(1)}, bf16[1024,128]{1,0:T(8,128)(2,1)S(1)}, u32[]{:S(2)}, u32[]{:S(2)}) %collective-permute-start.24) | collective-permute-done | bytes 262176 | tf_op jit(solution)/shard_map/ppermute | solution.py:29
  85.0 4.4 %collective-permute-done.25.refs_6_ = bf16[1024,128]{1,0:T(8,128)(2,1)S(1)} collective-permute-done((bf16[1024,128]{1,0:T(8,128)(2,1)S(1)}, bf16[1024,128]{1,0:T(8,128)(2,1)S(1)}, u32[]{:S(2)}, u32[]{:S(2)}) %collective-permute-start.25) | collective-permute-done | bytes 262176 | tf_op jit(solution)/shard_map/ppermute | solution.py:29
  89.4 1.3 %collective-permute-done.26.refs_7_ = bf16[1024,128]{1,0:T(8,128)(2,1)S(1)} collective-permute-done((bf16[1024,128]{1,0:T(8,128)(2,1)S(1)}, bf16[1024,128]{1,0:T(8,128)(2,1)S(1)}, u32[]{:S(2)}, u32[]{:S(2)}) %collective-permute-start.26) | collective-permute-done | bytes 262176 | tf_op jit(solution)/shard_map/ppermute | solution.py:29
  90.7 1.4 %finish.1 = f32[256,1024]{1,0:T(8,128)} custom-call(f32[2,1024,128]{2,1,0:T(8,128)S(1)} %get-tuple-element.27.sq_ref, f32[1024,128]{1,0:T(8,128)S(1)} %get-tuple-element.33.refs_0_, bf16[1024,128]{1,0:T(8,128)(2,1)S(1)} %collective-permute-done.18.refs_1_, bf16[1024,128]{1,0:T(8,128)(2,1)S(1)} %collective-permute-done.19.refs_2_, ...), custom_call_target="tpu_custom_call" | custom-call | tf_op jit(solution)/shard_map/finish/pallas_call | solution.py:296
  (16 shorter events, 0.0 us)
Async XLA Ops:
  2.3 17.0 %collective-permute-start = (bf16[2,528,128]{2,1,0:T(8,128)(2,1)}, bf16[2,528,128]{2,1,0:T(8,128)(2,1)S(1)}, u32[]{:S(2)}, u32[]{:S(2)}) collective-permute-start(bf16[2,528,128]{2,1,0:T(8,128)(2,1)} %get-tuple-element.25.refs_0_), channel_id=1, source_target_pairs={{0,32},{1,33},{2,34},{3,35},{4,36},{5,37},{6,38},{7,39},{8,40},{9,... | collective-permute-start | bytes 811016 | tf_op jit(solution)/shard_map/ppermute | solution.py:29
  4.4 7.2 %copy-start = (bf16[2,528,128]{2,1,0:T(8,128)(2,1)S(1)}, bf16[2,528,128]{2,1,0:T(8,128)(2,1)}, u32[]{:S(2)}) copy-start(bf16[2,528,128]{2,1,0:T(8,128)(2,1)} %get-tuple-element.25.refs_0_) | copy-start | bytes 811012
  4.4 26.7 %all-to-all-start = ((bf16[16,144,128]{2,1,0:T(8,128)(2,1)}), bf16[16,144,128]{2,1,0:T(8,128)(2,1)S(1)}, u32[]{:S(2)}, u32[]{:S(2)}) async-start(bf16[16,144,128]{2,1,0:T(8,128)(2,1)} %get-tuple-element.26), calls=%async_computation | async-start | bytes 1179648 | tf_op jit(solution)/shard_map/all_to_all | solution.py:312
  11.6 14.7 %collective-permute-start.1 = (bf16[2,528,128]{2,1,0:T(8,128)(2,1)S(1)}, bf16[2,528,128]{2,1,0:T(8,128)(2,1)S(1)}, u32[]{:S(2)}, u32[]{:S(2)}) collective-permute-start(bf16[2,528,128]{2,1,0:T(8,128)(2,1)S(1)} %copy-done), channel_id=1, source_target_pairs={{0,96},{1,97},{2,98},{3,99},{4,100},{5,101},{6,102},{7,103},{8,104... | collective-permute-start | bytes 811016 | tf_op jit(solution)/shard_map/ppermute | solution.py:29
  14.2 12.1 %collective-permute-start.2 = (bf16[2,528,128]{2,1,0:T(8,128)(2,1)S(1)}, bf16[2,528,128]{2,1,0:T(8,128)(2,1)S(1)}, u32[]{:S(2)}, u32[]{:S(2)}) collective-permute-start(bf16[2,528,128]{2,1,0:T(8,128)(2,1)S(1)} %copy-done), channel_id=1, source_target_pairs={{0,64},{1,65},{2,66},{3,67},{4,68},{5,69},{6,70},{7,71},{8,72},{9,... | collective-permute-start | bytes 811016 | tf_op jit(solution)/shard_map/ppermute | solution.py:29
  15.3 11.5 %collective-permute-start.7 = (bf16[2,528,128]{2,1,0:T(8,128)(2,1)S(1)}, bf16[2,528,128]{2,1,0:T(8,128)(2,1)S(1)}, u32[]{:S(2)}, u32[]{:S(2)}) collective-permute-start(bf16[2,528,128]{2,1,0:T(8,128)(2,1)S(1)} %copy-done), channel_id=1, source_target_pairs={{0,0},{1,1},{2,16},{3,17},{4,32},{5,33},{6,48},{7,49},{8,8},{9,9},... | collective-permute-start | bytes 811016 | tf_op jit(solution)/shard_map/ppermute | solution.py:29
  16.0 11.4 %collective-permute-start.3 = (bf16[2,528,128]{2,1,0:T(8,128)(2,1)S(1)}, bf16[2,528,128]{2,1,0:T(8,128)(2,1)S(1)}, u32[]{:S(2)}, u32[]{:S(2)}) collective-permute-start(bf16[2,528,128]{2,1,0:T(8,128)(2,1)S(1)} %copy-done), channel_id=1, source_target_pairs={{0,16},{1,17},{2,18},{3,19},{4,20},{5,21},{6,22},{7,23},{8,24},{9,... | collective-permute-start | bytes 811016 | tf_op jit(solution)/shard_map/ppermute | solution.py:29
  19.4 10.4 %collective-permute-start.4 = (bf16[2,528,128]{2,1,0:T(8,128)(2,1)S(1)}, bf16[2,528,128]{2,1,0:T(8,128)(2,1)S(1)}, u32[]{:S(2)}, u32[]{:S(2)}) collective-permute-start(bf16[2,528,128]{2,1,0:T(8,128)(2,1)S(1)} %collective-permute-done.refs_1_), channel_id=1, source_target_pairs={{0,16},{1,17},{2,18},{3,19},{4,20},{5,21},{6,22},{7,23},{8,24},{9,... | collective-permute-start | bytes 811016 | tf_op jit(solution)/shard_map/ppermute | solution.py:29
  26.3 4.7 %collective-permute-start.5 = (bf16[2,528,128]{2,1,0:T(8,128)(2,1)S(1)}, bf16[2,528,128]{2,1,0:T(8,128)(2,1)}, u32[]{:S(2)}, u32[]{:S(2)}) collective-permute-start(bf16[2,528,128]{2,1,0:T(8,128)(2,1)S(1)} %collective-permute-done.1.refs_2_), channel_id=1, source_target_pairs={{0,16},{1,17},{2,18},{3,19},{4,20},{5,21},{6,22},{7,23},{8,24},{9,... | collective-permute-start | bytes 811016 | tf_op jit(solution)/shard_map/ppermute | solution.py:29
  26.3 4.7 %collective-permute-start.6 = (bf16[2,528,128]{2,1,0:T(8,128)(2,1)S(1)}, bf16[2,528,128]{2,1,0:T(8,128)(2,1)}, u32[]{:S(2)}, u32[]{:S(2)}) collective-permute-start(bf16[2,528,128]{2,1,0:T(8,128)(2,1)S(1)} %collective-permute-done.2.refs_3_), channel_id=1, source_target_pairs={{0,16},{1,17},{2,18},{3,19},{4,20},{5,21},{6,22},{7,23},{8,24},{9,... | collective-permute-start | bytes 811016 | tf_op jit(solution)/shard_map/ppermute | solution.py:29
  26.9 17.7 %collective-permute-start.8 = (bf16[2,528,128]{2,1,0:T(8,128)(2,1)S(1)}, bf16[2,528,128]{2,1,0:T(8,128)(2,1)S(1)}, u32[]{:S(2)}, u32[]{:S(2)}) collective-permute-start(bf16[2,528,128]{2,1,0:T(8,128)(2,1)S(1)} %collective-permute-done.7.refs_0_), channel_id=1, source_target_pairs={{0,32},{1,33},{2,34},{3,35},{4,36},{5,37},{6,38},{7,39},{8,40},{9,... | collective-permute-start | bytes 811016 | tf_op jit(solution)/shard_map/ppermute | solution.py:29
  27.4 17.4 %collective-permute-start.9 = (bf16[2,528,128]{2,1,0:T(8,128)(2,1)S(1)}, bf16[2,528,128]{2,1,0:T(8,128)(2,1)S(1)}, u32[]{:S(2)}, u32[]{:S(2)}) collective-permute-start(bf16[2,528,128]{2,1,0:T(8,128)(2,1)S(1)} %collective-permute-done.7.refs_0_), channel_id=1, source_target_pairs={{0,96},{1,97},{2,98},{3,99},{4,100},{5,101},{6,102},{7,103},{8,104... | collective-permute-start | bytes 811016 | tf_op jit(solution)/shard_map/ppermute | solution.py:29
  29.8 15.3 %collective-permute-start.10 = (bf16[2,528,128]{2,1,0:T(8,128)(2,1)S(1)}, bf16[2,528,128]{2,1,0:T(8,128)(2,1)S(1)}, u32[]{:S(2)}, u32[]{:S(2)}) collective-permute-start(bf16[2,528,128]{2,1,0:T(8,128)(2,1)S(1)} %collective-permute-done.7.refs_0_), channel_id=1, source_target_pairs={{0,64},{1,65},{2,66},{3,67},{4,68},{5,69},{6,70},{7,71},{8,72},{9,... | collective-permute-start | bytes 811016 | tf_op jit(solution)/shard_map/ppermute | solution.py:29
  35.2 9.1 %collective-permute-start.11 = (bf16[1024,128]{1,0:T(8,128)(2,1)S(1)}, bf16[1024,128]{1,0:T(8,128)(2,1)S(1)}, u32[]{:S(2)}, u32[]{:S(2)}) collective-permute-start(bf16[1024,128]{1,0:T(8,128)(2,1)S(1)} %get-tuple-element.28.refs_8_), channel_id=1, source_target_pairs={{0,8},{1,9},{2,10},{3,11},{4,12},{5,13},{6,14},{7,15},{8,0},{9,1},... | collective-permute-start | bytes 786440 | tf_op jit(solution)/shard_map/ppermute | solution.py:29
  36.9 9.9 %collective-permute-start.16 = (bf16[1024,128]{1,0:T(8,128)(2,1)S(1)}, bf16[1024,128]{1,0:T(8,128)(2,1)S(1)}, u32[]{:S(2)}, u32[]{:S(2)}) collective-permute-start(bf16[1024,128]{1,0:T(8,128)(2,1)S(1)} %get-tuple-element.28.refs_8_), channel_id=1, source_target_pairs={{0,9},{1,8},{2,11},{3,10},{4,13},{5,12},{6,15},{7,14},{8,1},{9,0},... | collective-permute-start | bytes 786440 | tf_op jit(solution)/shard_map/ppermute | solution.py:29
  44.3 12.4 %collective-permute-start.12 = (bf16[2,528,128]{2,1,0:T(8,128)(2,1)S(1)}, bf16[2,528,128]{2,1,0:T(8,128)(2,1)S(1)}, u32[]{:S(2)}, u32[]{:S(2)}) collective-permute-start(bf16[2,528,128]{2,1,0:T(8,128)(2,1)S(1)} %collective-permute-done.7.refs_0_), channel_id=1, source_target_pairs={{0,16},{1,17},{2,18},{3,19},{4,20},{5,21},{6,22},{7,23},{8,24},{9,... | collective-permute-start | bytes 811016 | tf_op jit(solution)/shard_map/ppermute | solution.py:29
  44.6 14.0 %collective-permute-start.13 = (bf16[2,528,128]{2,1,0:T(8,128)(2,1)S(1)}, bf16[2,528,128]{2,1,0:T(8,128)(2,1)S(1)}, u32[]{:S(2)}, u32[]{:S(2)}) collective-permute-start(bf16[2,528,128]{2,1,0:T(8,128)(2,1)S(1)} %collective-permute-done.8.refs_1_), channel_id=1, source_target_pairs={{0,16},{1,17},{2,18},{3,19},{4,20},{5,21},{6,22},{7,23},{8,24},{9,... | collective-permute-start | bytes 811016 | tf_op jit(solution)/shard_map/ppermute | solution.py:29
  44.9 15.5 %collective-permute-start.14 = (bf16[2,528,128]{2,1,0:T(8,128)(2,1)S(1)}, bf16[2,528,128]{2,1,0:T(8,128)(2,1)S(1)}, u32[]{:S(2)}, u32[]{:S(2)}) collective-permute-start(bf16[2,528,128]{2,1,0:T(8,128)(2,1)S(1)} %collective-permute-done.9.refs_2_), channel_id=1, source_target_pairs={{0,16},{1,17},{2,18},{3,19},{4,20},{5,21},{6,22},{7,23},{8,24},{9,... | collective-permute-start | bytes 811016 | tf_op jit(solution)/shard_map/ppermute | solution.py:29
  45.1 15.3 %collective-permute-start.15 = (bf16[2,528,128]{2,1,0:T(8,128)(2,1)S(1)}, bf16[2,528,128]{2,1,0:T(8,128)(2,1)S(1)}, u32[]{:S(2)}, u32[]{:S(2)}) collective-permute-start(bf16[2,528,128]{2,1,0:T(8,128)(2,1)S(1)} %collective-permute-done.10.refs_3_), channel_id=1, source_target_pairs={{0,16},{1,17},{2,18},{3,19},{4,20},{5,21},{6,22},{7,23},{8,24},{9,... | collective-permute-start | bytes 811016 | tf_op jit(solution)/shard_map/ppermute | solution.py:29
  46.8 9.4 %collective-permute-start.17 = (bf16[1024,128]{1,0:T(8,128)(2,1)S(1)}, bf16[1024,128]{1,0:T(8,128)(2,1)S(1)}, u32[]{:S(2)}, u32[]{:S(2)}) collective-permute-start(bf16[1024,128]{1,0:T(8,128)(2,1)S(1)} %get-tuple-element.28.refs_8_), channel_id=1, source_target_pairs={{0,1},{1,0},{2,3},{3,2},{4,5},{5,4},{6,7},{7,6},{8,9},{9,8},{10,11... | collective-permute-start | bytes 786440 | tf_op jit(solution)/shard_map/ppermute | solution.py:29
  56.3 12.4 %collective-permute-start.21 = (bf16[1024,128]{1,0:T(8,128)(2,1)S(1)}, bf16[1024,128]{1,0:T(8,128)(2,1)S(1)}, u32[]{:S(2)}, u32[]{:S(2)}) collective-permute-start(bf16[1024,128]{1,0:T(8,128)(2,1)S(1)} %get-tuple-element.40.refs_8_), channel_id=1, source_target_pairs={{0,8},{1,9},{2,10},{3,11},{4,12},{5,13},{6,14},{7,15},{8,0},{9,1},... | collective-permute-start | bytes 786440 | tf_op jit(solution)/shard_map/ppermute | solution.py:29
  56.8 14.0 %collective-permute-start.22 = (bf16[1024,128]{1,0:T(8,128)(2,1)S(1)}, bf16[1024,128]{1,0:T(8,128)(2,1)S(1)}, u32[]{:S(2)}, u32[]{:S(2)}) collective-permute-start(bf16[1024,128]{1,0:T(8,128)(2,1)S(1)} %get-tuple-element.40.refs_8_), channel_id=1, source_target_pairs={{0,9},{1,8},{2,11},{3,10},{4,13},{5,12},{6,15},{7,14},{8,1},{9,0},... | collective-permute-start | bytes 786440 | tf_op jit(solution)/shard_map/ppermute | solution.py:29
  58.6 12.2 %collective-permute-start.23 = (bf16[1024,128]{1,0:T(8,128)(2,1)S(1)}, bf16[1024,128]{1,0:T(8,128)(2,1)S(1)}, u32[]{:S(2)}, u32[]{:S(2)}) collective-permute-start(bf16[1024,128]{1,0:T(8,128)(2,1)S(1)} %get-tuple-element.40.refs_8_), channel_id=1, source_target_pairs={{0,1},{1,0},{2,3},{3,2},{4,5},{5,4},{6,7},{7,6},{8,9},{9,8},{10,11... | collective-permute-start | bytes 786440 | tf_op jit(solution)/shard_map/ppermute | solution.py:29
  65.2 14.8 %collective-permute-start.18 = (bf16[1024,128]{1,0:T(8,128)(2,1)S(1)}, bf16[1024,128]{1,0:T(8,128)(2,1)S(1)}, u32[]{:S(2)}, u32[]{:S(2)}) collective-permute-start(bf16[1024,128]{1,0:T(8,128)(2,1)S(1)} %get-tuple-element.34), channel_id=1, source_target_pairs={{0,2},{1,3},{2,0},{3,1},{4,6},{5,7},{6,4},{7,5},{8,10},{9,11},{10,... | collective-permute-start | bytes 786440 | tf_op jit(solution)/shard_map/ppermute | solution.py:29
  65.3 15.3 %collective-permute-start.19 = (bf16[1024,128]{1,0:T(8,128)(2,1)S(1)}, bf16[1024,128]{1,0:T(8,128)(2,1)S(1)}, u32[]{:S(2)}, u32[]{:S(2)}) collective-permute-start(bf16[1024,128]{1,0:T(8,128)(2,1)S(1)} %get-tuple-element.35), channel_id=1, source_target_pairs={{0,6},{1,7},{2,4},{3,5},{4,2},{5,3},{6,0},{7,1},{8,14},{9,15},{10,... | collective-permute-start | bytes 786440 | tf_op jit(solution)/shard_map/ppermute | solution.py:29
  68.7 11.9 %collective-permute-start.20 = (bf16[1024,128]{1,0:T(8,128)(2,1)S(1)}, bf16[1024,128]{1,0:T(8,128)(2,1)S(1)}, u32[]{:S(2)}, u32[]{:S(2)}) collective-permute-start(bf16[1024,128]{1,0:T(8,128)(2,1)S(1)} %get-tuple-element.36), channel_id=1, source_target_pairs={{0,4},{1,5},{2,6},{3,7},{4,0},{5,1},{6,2},{7,3},{8,12},{9,13},{10,... | collective-permute-start | bytes 786440 | tf_op jit(solution)/shard_map/ppermute | solution.py:29
  75.6 9.4 %collective-permute-start.24 = (bf16[1024,128]{1,0:T(8,128)(2,1)S(1)}, bf16[1024,128]{1,0:T(8,128)(2,1)S(1)}, u32[]{:S(2)}, u32[]{:S(2)}) collective-permute-start(bf16[1024,128]{1,0:T(8,128)(2,1)S(1)} %get-tuple-element.42), channel_id=1, source_target_pairs={{0,2},{1,3},{2,0},{3,1},{4,6},{5,7},{6,4},{7,5},{8,10},{9,11},{10,... | collective-permute-start | bytes 786440 | tf_op jit(solution)/shard_map/ppermute | solution.py:29
  76.3 13.1 %collective-permute-start.25 = (bf16[1024,128]{1,0:T(8,128)(2,1)S(1)}, bf16[1024,128]{1,0:T(8,128)(2,1)S(1)}, u32[]{:S(2)}, u32[]{:S(2)}) collective-permute-start(bf16[1024,128]{1,0:T(8,128)(2,1)S(1)} %get-tuple-element.43), channel_id=1, source_target_pairs={{0,6},{1,7},{2,4},{3,5},{4,2},{5,3},{6,0},{7,1},{8,14},{9,15},{10,... | collective-permute-start | bytes 786440 | tf_op jit(solution)/shard_map/ppermute | solution.py:29
  80.0 10.8 %collective-permute-start.26 = (bf16[1024,128]{1,0:T(8,128)(2,1)S(1)}, bf16[1024,128]{1,0:T(8,128)(2,1)S(1)}, u32[]{:S(2)}, u32[]{:S(2)}) collective-permute-start(bf16[1024,128]{1,0:T(8,128)(2,1)S(1)} %get-tuple-element.44), channel_id=1, source_target_pairs={{0,4},{1,5},{2,6},{3,7},{4,0},{5,1},{6,2},{7,3},{8,12},{9,13},{10,... | collective-permute-start | bytes 786440 | tf_op jit(solution)/shard_map/ppermute | solution.py:29

commit v3 on v2

--- a/solution.py
+++ b/solution.py
@@ -215,92 +215,98 @@
     )(where, *ring, *other, slab)
 
 
-def cube_kernel(place_ref, *refs):
-    ring, other, squares, outs = refs[:4], refs[4:8], refs[8:12], refs[12:16]
-    panel, sq, acc, ints, scal, sem = refs[16:]
-    x, y = place_ref[2], place_ref[3]
-    copies = fetch_rows(place_ref, ring, other, panel, sem)
-    more = []
-    for n, part in enumerate(squares):
-        more.append(pltpu.make_async_copy(part, sq.at[x ^ FLIPS[n]], sem.at[8 + n]))
-    for copy in more:
-        copy.start()
-    acc[...] = jnp.zeros_like(acc)
-    for copy in copies:
-        copy.wait()
-    read_columns(panel, ints)
-    to_scal = pltpu.make_async_copy(ints, scal, sem.at[0])
+def columns_kernel(same, other, scal, ints, sem):
+    for b, ref in enumerate((same, other)):
+        for n in range(8):
+            row = ref[n // 2, n % 2, 512:528, :].astype(F32)[0:1, :]
+            ints[8 * b + n : 8 * b + n + 1, :] = row.astype(I32)
+    to_scal = pltpu.make_async_copy(ints, scal, sem)
     to_scal.start()
     to_scal.wait()
-    for copy in more:
-        copy.wait()
+
+
+def columns_of(same, other):
+    return pl.pallas_call(
+        columns_kernel,
+        out_shape=jax.ShapeDtypeStruct((16, 128), I32),
+        in_specs=[VMEM, VMEM],
+        out_specs=SMEM,
+        scratch_shapes=[pltpu.VMEM((16, 128), I32), pltpu.SemaphoreType.DMA],
+        compiler_params=PARAMS,
+        name="columns",
+    )(same, other)
+
+
+def cube_kernel(place_ref, scal, same, other, *refs):
+    squares, outs, (acc,) = refs[:4], refs[4:8], refs[8:]
+    z, core, x, y = (place_ref[n] for n in range(4))
+    acc[...] = jnp.zeros_like(acc)
     quarter = lane_masks()
     masks = [(quarter == n).astype(F32).astype(BF16) for n in range(4)]
 
-    def step(n, carry):
-        source, quad = lax.div(n, 4), lax.rem(n, 4)
-        right = sq[source, pl.ds(pl.multiple_of(quad * 256, 256), 256), :]
-        rows = pl.ds(pl.multiple_of(quad * 128, 128), 128)
-        for there in range(4):
-            half_row = 8 * lax.rem(source, 2) + 2 * there + lax.div(source, 2)
-            t = panel[half_row, rows, :]
-            t = jnp.concatenate([t[0:64], t[64:128]], axis=1)
-            left = jnp.concatenate([t * mask for mask in masks], axis=0)
-            out = jnp.dot(left, right, preferred_element_type=F32)
-            for c4 in range(4):
-                j = lax.rem(scal[half_row, quad * 4 + c4], 16)
-                into = pl.ds(pl.multiple_of(j * 64, 64), 64)
-                acc[there, into, :] += out[c4 * 64 : c4 * 64 + 64, :]
-        return carry
-
-    lax.fori_loop(0, 16, step, 0, unroll=4)
+    for n in range(4):
+        source = x ^ FLIPS[n]
+        half = lax.div(source, 2)
+
+        def step(quad, carry, n=n, source=source, half=half):
+            right = squares[n][pl.ds(pl.multiple_of(quad * 256, 256), 256), :]
+            rows = pl.ds(pl.multiple_of(quad * 128, 128), 128)
+            for b, panel in enumerate((same, other)):
+                for m in range(2):
+                    there = 2 * m + (core ^ b)
+                    flip = z ^ (2 * lax.rem(source, 2) + m)
+                    at = flip ^ lax.div(flip, 2)
+                    t = panel[at, half, rows, :]
+                    t = jnp.concatenate([t[0:64], t[64:128]], axis=1)
+                    left = jnp.concatenate([t * mask for mask in masks], axis=0)
+                    out = jnp.dot(left, right, preferred_element_type=F32)
+                    for c4 in range(4):
+                        j = lax.rem(scal[8 * b + 2 * at + half, quad * 4 + c4], 16)
+                        into = pl.ds(pl.multiple_of(j * 64, 64), 64)
+                        acc[there, into, :] += out[c4 * 64 : c4 * 64 + 64, :]
+            return carry
+
+        lax.fori_loop(0, 4, step, 0, unroll=True)
     for n, out in enumerate(outs):
         out[...] = acc[y ^ FLIPS[n]].astype(out.dtype)
 
 
-def cube_of(where, ring, other, squares):
+def cube_of(where, columns, same, other, squares):
     return pl.pallas_call(
         cube_kernel,
         out_shape=(
             jax.ShapeDtypeStruct((1024, 128), F32),
             *[jax.ShapeDtypeStruct((1024, 128), BF16)] * 3,
         ),
-        in_specs=[SMEM] + [ANY] * 12,
+        in_specs=[SMEM, SMEM] + [VMEM] * 6,
         out_specs=(VMEM,) * 4,
-        scratch_shapes=[
-            pltpu.VMEM((16, HALF, 128), BF16),
-            pltpu.VMEM((4, 1024, 128), BF16),
-            pltpu.VMEM((4, 1024, 128), F32),
-            pltpu.VMEM((16, 128), I32),
-            pltpu.SMEM((16, 128), I32),
-            pltpu.SemaphoreType.DMA((12,)),
-        ],
+        scratch_shapes=[pltpu.VMEM((4, 1024, 128), F32)],
         compiler_params=PARAMS,
         name="cube",
-    )(where, *ring, *other, *squares)
-
-
-def finish_kernel(sq_ref, *refs):
-    out_ref = refs[8]
+    )(where, columns, same, other, *squares)
+
+
+def finish_kernel(h, sq_ref, own_ref, a_ref, b_ref, c_ref, *refs):
+    out_ref = refs[-1]
     for m in range(8):
         at = pl.ds(m * 128, 128)
-        for h in range(2):
-            cube = refs[4 * h][at, :]
-            for ref in refs[4 * h + 1 : 4 * h + 4]:
-                cube += ref[at, :].astype(F32)
-            total = 3.0 * sq_ref[h, at, :] - 2.0 * cube
-            out_ref[h * 128 : h * 128 + 128, at] = jnp.transpose(total)
-
-
-def finish(square32, cubes):
-    return pl.pallas_call(
-        finish_kernel,
+        cube = own_ref[at, :]
+        for ref in (a_ref, b_ref, c_ref):
+            cube += ref[at, :].astype(F32)
+        out_ref[:, at] = jnp.transpose(3.0 * sq_ref[h, at, :] - 2.0 * cube)
+
+
+def finish(h, square32, cubes, before):
+    return pl.pallas_call(
+        functools.partial(finish_kernel, h),
         out_shape=jax.ShapeDtypeStruct((256, 1024), F32),
-        in_specs=[VMEM] * 9,
-        out_specs=VMEM,
+        grid=(1,),
+        in_specs=[VMEM] * 5 + [ANY] * len(before),
+        out_specs=pl.BlockSpec((128, 1024), lambda i: (h, 0)),
+        input_output_aliases={5: 0} if before else {},
         compiler_params=PARAMS,
         name="finish",
-    )(square32, *cubes)
+    )(square32, *cubes, *before)
 
 
 def body(blocks, pattern):
@@ -317,12 +323,15 @@
     for mine in squares:
         moved = [swap(after(mine, *first), x=d) for d, first in zip(FLIPS[1:], moved)]
         if turned_other is None:
-            turned_other = [swap(after(v, moved[0]), core=1) for v in turned_ring]
-        own, *outs = cube_of(where, turned_ring, turned_other, [mine, *moved])
+            turned = jnp.stack(turned_ring)
+            turned_other = swap(after(turned, *moved), core=1)
+            columns = columns_of(turned, turned_other)
+        own, *outs = cube_of(where, columns, turned, turned_other, [mine, *moved])
         moved = [(v,) for v in moved]
         outs = [swap(v, y=d) for v, d in zip(outs, FLIPS[1:])]
-        cubes += [own, *outs]
-    return finish(square32, cubes)
+        cubes.append([own, *outs])
+    first = finish(0, square32, cubes[0], [])
+    return finish(1, square32, cubes[1], [first])
 
 
 def solution(mesh):

time: 92.4 us -> 88.6 us (0.959)
  waiting for transfers between devices: 33.3 us -> 30.9 us
  Pallas kernels: 17.4 us -> 16 us
  other arithmetic: 0.08 us -> 1.25 us
  starting transfers between devices: 41.2 us -> 40.1 us
    pallas_call x2, Pallas kernels: 9.61 us -> 6.82 us  [cube_of(): pl.pallas_call(cube_kernel, out_shape=(jax.ShapeDtypeStruct((1024, 128),...]
    ppermute x27 -> x24, waiting for transfers between devices: 33.3 us -> 30.9 us  [permute(): return lax.ppermute(value, AXES, pairs)]
    pallas_call x1 -> x3, Pallas kernels: 1.38 us -> 3.44 us  [the longest x2 2.03 us: finish(): pl.pallas_call(functools.partial(finish_kernel, h), out_shape=jax.ShapeDt...]
    another operation x0 -> x1, other arithmetic: none -> 1.17 us  [body(): turned = jnp.stack(turned_ring)]
    ppermute x27 -> x24, starting transfers between devices: 34 us -> 33 us  [permute(): return lax.ppermute(value, AXES, pairs)]
  transfers between devices with their start and end apart: 28 -> 25, of which waited for: 8 -> 9; matrix products, arithmetic and copies ran while one was open for 0% -> 1% of each run, Pallas kernels for 15% -> 14%
where the time goes in v3:
time: 88.6 us; the launch traced here: 88.3 us
  starting transfers between devices  40.1 us (45%)
  waiting for transfers between devices  30.9 us (35%)
  Pallas kernels  16 us (18%)
  other arithmetic  1.25 us (1%)
    ppermute x24, starting transfers between devices, permute(): return lax.ppermute(value, AXES, pairs)  33 us
    ppermute x24, waiting for transfers between devices, permute(): return lax.ppermute(value, AXES, pairs)  30.9 us
    all_to_all x1, starting transfers between devices, body(): slab = lax.all_to_all(slab, ('col', 'depth'), 0, 0, tiled=True)  7.03 us
    pallas_call x2, Pallas kernels, cube_of(): pl.pallas_call(cube_kernel, out_shape=(jax.ShapeDtypeStruct((1024, 128),...  6.82 us
    pallas_call x1, Pallas kernels, square_of(): pl.pallas_call(square_kernel, out_shape=(jax.ShapeDtypeStruct((2, 1024, 1...  3.41 us
    pallas_call x1, Pallas kernels, pack(): pl.pallas_call(pack_kernel, out_shape=(jax.ShapeDtypeStruct((2, HALF, 128...  2.31 us
    pallas_call x2, Pallas kernels, finish(): pl.pallas_call(functools.partial(finish_kernel, h), out_shape=jax.ShapeDt...  2.03 us
  transfers between devices with their start and end apart: 25, of which 9 were waited for; matrix products, arithmetic and copies ran while one was open for 1% of the time, Pallas kernels for 14%

profile of v3, /device:TPU:0, one launch (start us, length us, event | category | flops | bytes accessed | tf_op | source)
XLA Modules:
  0.0 88.3 jit_solution(10564986956157062420)
XLA Ops:
  0.0 2.3 %pack.1 = (bf16[2,528,128]{2,1,0:T(8,128)(2,1)}, bf16[16,144,128]{2,1,0:T(8,128)(2,1)}) custom-call(bf16[32,4096]{1,0:T(8,128)(2,1)} %bitcast.12, s32[1,32]{1,0:T(1,128)} %bitcast.13), custom_call_target="tpu_custom_call" | custom-call | tf_op jit(solution)/shard_map/pack/pallas_call | solution.py:109
  2.3 2.1 %collective-permute-start = (bf16[2,528,128]{2,1,0:T(8,128)(2,1)}, bf16[2,528,128]{2,1,0:T(8,128)(2,1)S(1)}, u32[]{:S(2)}, u32[]{:S(2)}) collective-permute-start(bf16[2,528,128]{2,1,0:T(8,128)(2,1)} %get-tuple-element.22.refs_0_), channel_id=1, source_target_pairs={{0,32},{1,33},{2,34},{3,35},{4,36},{5,37},{6,38},{7,39},{8,40},{9,... | collective-permute-start | bytes 811016 | tf_op jit(solution)/shard_map/ppermute | solution.py:29
  4.4 7.0 %all-to-all-start = ((bf16[16,144,128]{2,1,0:T(8,128)(2,1)}), bf16[16,144,128]{2,1,0:T(8,128)(2,1)S(1)}, u32[]{:S(2)}, u32[]{:S(2)}) async-start(bf16[16,144,128]{2,1,0:T(8,128)(2,1)} %get-tuple-element.23), calls=%async_computation | async-start | bytes 1179648 | tf_op jit(solution)/shard_map/all_to_all | solution.py:318
  11.5 2.6 %collective-permute-start.1 = (bf16[2,528,128]{2,1,0:T(8,128)(2,1)S(1)}, bf16[2,528,128]{2,1,0:T(8,128)(2,1)S(1)}, u32[]{:S(2)}, u32[]{:S(2)}) collective-permute-start(bf16[2,528,128]{2,1,0:T(8,128)(2,1)S(1)} %copy-done), channel_id=1, source_target_pairs={{0,96},{1,97},{2,98},{3,99},{4,100},{5,101},{6,102},{7,103},{8,104... | collective-permute-start | bytes 811016 | tf_op jit(solution)/shard_map/ppermute | solution.py:29
  14.1 1.2 %collective-permute-start.2 = (bf16[2,528,128]{2,1,0:T(8,128)(2,1)S(1)}, bf16[2,528,128]{2,1,0:T(8,128)(2,1)S(1)}, u32[]{:S(2)}, u32[]{:S(2)}) collective-permute-start(bf16[2,528,128]{2,1,0:T(8,128)(2,1)S(1)} %copy-done), channel_id=1, source_target_pairs={{0,64},{1,65},{2,66},{3,67},{4,68},{5,69},{6,70},{7,71},{8,72},{9,... | collective-permute-start | bytes 811016 | tf_op jit(solution)/shard_map/ppermute | solution.py:29
  15.2 0.7 collective-permute-start.7
  15.9 3.3 %collective-permute-start.3 = (bf16[2,528,128]{2,1,0:T(8,128)(2,1)S(1)}, bf16[2,528,128]{2,1,0:T(8,128)(2,1)S(1)}, u32[]{:S(2)}, u32[]{:S(2)}) collective-permute-start(bf16[2,528,128]{2,1,0:T(8,128)(2,1)S(1)} %copy-done), channel_id=1, source_target_pairs={{0,16},{1,17},{2,18},{3,19},{4,20},{5,21},{6,22},{7,23},{8,24},{9,... | collective-permute-start | bytes 811016 | tf_op jit(solution)/shard_map/ppermute | solution.py:29
  19.2 0.0 collective-permute-done.refs_1_
  19.2 0.1 collective-permute-start.4
  19.3 6.9 %collective-permute-done.1.refs_2_ = bf16[2,528,128]{2,1,0:T(8,128)(2,1)S(1)} collective-permute-done((bf16[2,528,128]{2,1,0:T(8,128)(2,1)S(1)}, bf16[2,528,128]{2,1,0:T(8,128)(2,1)S(1)}, u32[]{:S(2)}, u32[]{:S(2)}) %collective-permute-start.1) | collective-permute-done | bytes 270368 | tf_op jit(solution)/shard_map/ppermute | solution.py:29
  26.2 0.0 collective-permute-start.5
  26.2 0.0 collective-permute-done.2.refs_3_
  26.2 0.5 collective-permute-start.6
  26.7 0.0 collective-permute-done.7
  26.7 0.6 collective-permute-start.8
  27.3 0.0 collective-permute-done.3.refs_4_
  27.3 2.3 %collective-permute-start.9 = (bf16[2,528,128]{2,1,0:T(8,128)(2,1)S(1)}, bf16[2,528,128]{2,1,0:T(8,128)(2,1)}, u32[]{:S(2)}, u32[]{:S(2)}) collective-permute-start(bf16[2,528,128]{2,1,0:T(8,128)(2,1)S(1)} %collective-permute-done.7), channel_id=1, source_target_pairs={{0,96},{1,97},{2,98},{3,99},{4,100},{5,101},{6,102},{7,103},{8,104... | collective-permute-start | bytes 811016 | tf_op jit(solution)/shard_map/ppermute | solution.py:29
  29.7 0.0 collective-permute-done.4.refs_5_
  29.7 1.2 %collective-permute-start.10 = (bf16[2,528,128]{2,1,0:T(8,128)(2,1)S(1)}, bf16[2,528,128]{2,1,0:T(8,128)(2,1)}, u32[]{:S(2)}, u32[]{:S(2)}) collective-permute-start(bf16[2,528,128]{2,1,0:T(8,128)(2,1)S(1)} %collective-permute-done.7), channel_id=1, source_target_pairs={{0,64},{1,65},{2,66},{3,67},{4,68},{5,69},{6,70},{7,71},{8,72},{9,... | collective-permute-start | bytes 811016 | tf_op jit(solution)/shard_map/ppermute | solution.py:29
  30.9 0.1 pad_add_fusion.place_ref
  30.9 0.0 collective-permute-done.5.refs_6_
  30.9 3.4 %square.1 = (f32[2,1024,128]{2,1,0:T(8,128)S(1)}, bf16[1024,128]{1,0:T(8,128)(2,1)S(1)}, bf16[1024,128]{1,0:T(8,128)(2,1)S(1)}) custom-call(s32[4]{0:T(128)S(1)} %pad_add_fusion.place_ref, bf16[2,528,128]{2,1,0:T(8,128)(2,1)S(1)} %copy-done, bf16[2,528,128]{2,1,0:T(8,128)(2,1)S(1)} %collective-permute-done.refs_1_, ...), custom_call_target="tpu_custom_call" | custom-call | tf_op jit(solution)/shard_map/square/pallas_call | solution.py:198
  34.4 1.7 %collective-permute-start.11 = (bf16[1024,128]{1,0:T(8,128)(2,1)S(1)}, bf16[1024,128]{1,0:T(8,128)(2,1)S(1)}, u32[]{:S(2)}, u32[]{:S(2)}) collective-permute-start(bf16[1024,128]{1,0:T(8,128)(2,1)S(1)} %get-tuple-element.25.refs_0_), channel_id=1, source_target_pairs={{0,8},{1,9},{2,10},{3,11},{4,12},{5,13},{6,14},{7,15},{8,0},{9,1},... | collective-permute-start | bytes 786440 | tf_op jit(solution)/shard_map/ppermute | solution.py:29
  36.1 2.1 %collective-permute-start.12 = (bf16[1024,128]{1,0:T(8,128)(2,1)S(1)}, bf16[1024,128]{1,0:T(8,128)(2,1)S(1)}, u32[]{:S(2)}, u32[]{:S(2)}) collective-permute-start(bf16[1024,128]{1,0:T(8,128)(2,1)S(1)} %get-tuple-element.25.refs_0_), channel_id=1, source_target_pairs={{0,9},{1,8},{2,11},{3,10},{4,13},{5,12},{6,15},{7,14},{8,1},{9,0},... | collective-permute-start | bytes 786440 | tf_op jit(solution)/shard_map/ppermute | solution.py:29
  38.1 1.1 %collective-permute-start.13 = (bf16[1024,128]{1,0:T(8,128)(2,1)S(1)}, bf16[1024,128]{1,0:T(8,128)(2,1)S(1)}, u32[]{:S(2)}, u32[]{:S(2)}) collective-permute-start(bf16[1024,128]{1,0:T(8,128)(2,1)S(1)} %get-tuple-element.25.refs_0_), channel_id=1, source_target_pairs={{0,1},{1,0},{2,3},{3,2},{4,5},{5,4},{6,7},{7,6},{8,9},{9,8},{10,11... | collective-permute-start | bytes 786440 | tf_op jit(solution)/shard_map/ppermute | solution.py:29
  39.2 2.7 %collective-permute-done.9 = bf16[2,528,128]{2,1,0:T(8,128)(2,1)} collective-permute-done((bf16[2,528,128]{2,1,0:T(8,128)(2,1)S(1)}, bf16[2,528,128]{2,1,0:T(8,128)(2,1)}, u32[]{:S(2)}, u32[]{:S(2)}) %collective-permute-start.9) | collective-permute-done | bytes 270368 | tf_op jit(solution)/shard_map/ppermute | solution.py:29
  41.9 1.5 %collective-permute-done.10 = bf16[2,528,128]{2,1,0:T(8,128)(2,1)} collective-permute-done((bf16[2,528,128]{2,1,0:T(8,128)(2,1)S(1)}, bf16[2,528,128]{2,1,0:T(8,128)(2,1)}, u32[]{:S(2)}, u32[]{:S(2)}) %collective-permute-start.10) | collective-permute-done | bytes 270368 | tf_op jit(solution)/shard_map/ppermute | solution.py:29
  43.3 1.2 %pad_maximum_fusion.same = bf16[4,2,528,128]{3,2,1,0:T(8,128)(2,1)S(1)} fusion(bf16[1,2,528,128]{3,2,1,0:T(8,128)(2,1)} %bitcast.9, bf16[1,2,528,128]{3,2,1,0:T(8,128)(2,1)} %bitcast.8, bf16[1,2,528,128]{3,2,1,0:T(8,128)(2,1)S(1)} %bitcast.11, bf16[1,2,528,128]{3,2,1,0:T(8,128)(2,1)S(1)} %bitcast.10), kind=kLoop, calls=%fused_computation | loop fusion | flops 1622016 | bytes 2162688 | tf_op jit(solution)/shard_map/stack | solution.py:326
  44.5 7.1 %collective-permute-done.12.refs_2_ = bf16[1024,128]{1,0:T(8,128)(2,1)S(1)} collective-permute-done((bf16[1024,128]{1,0:T(8,128)(2,1)S(1)}, bf16[1024,128]{1,0:T(8,128)(2,1)S(1)}, u32[]{:S(2)}, u32[]{:S(2)}) %collective-permute-start.12) | collective-permute-done | bytes 262176 | tf_op jit(solution)/shard_map/ppermute | solution.py:29
  51.6 1.3 %collective-permute-start.17 = (bf16[1024,128]{1,0:T(8,128)(2,1)S(1)}, bf16[1024,128]{1,0:T(8,128)(2,1)S(1)}, u32[]{:S(2)}, u32[]{:S(2)}) collective-permute-start(bf16[1024,128]{1,0:T(8,128)(2,1)S(1)} %get-tuple-element.30.refs_0_), channel_id=1, source_target_pairs={{0,1},{1,0},{2,3},{3,2},{4,5},{5,4},{6,7},{7,6},{8,9},{9,8},{10,11... | collective-permute-start | bytes 786440 | tf_op jit(solution)/shard_map/ppermute | solution.py:29
  52.9 1.1 %collective-permute-start.16 = (bf16[1024,128]{1,0:T(8,128)(2,1)S(1)}, bf16[1024,128]{1,0:T(8,128)(2,1)S(1)}, u32[]{:S(2)}, u32[]{:S(2)}) collective-permute-start(bf16[1024,128]{1,0:T(8,128)(2,1)S(1)} %get-tuple-element.30.refs_0_), channel_id=1, source_target_pairs={{0,9},{1,8},{2,11},{3,10},{4,13},{5,12},{6,15},{7,14},{8,1},{9,0},... | collective-permute-start | bytes 786440 | tf_op jit(solution)/shard_map/ppermute | solution.py:29
  54.0 1.1 %collective-permute-start.15 = (bf16[1024,128]{1,0:T(8,128)(2,1)S(1)}, bf16[1024,128]{1,0:T(8,128)(2,1)S(1)}, u32[]{:S(2)}, u32[]{:S(2)}) collective-permute-start(bf16[1024,128]{1,0:T(8,128)(2,1)S(1)} %get-tuple-element.30.refs_0_), channel_id=1, source_target_pairs={{0,8},{1,9},{2,10},{3,11},{4,12},{5,13},{6,14},{7,15},{8,0},{9,1},... | collective-permute-start | bytes 786440 | tf_op jit(solution)/shard_map/ppermute | solution.py:29
  55.1 1.4 %columns.1.scal = s32[16,128]{1,0:T(8,128)S(1)} custom-call(bf16[4,2,528,128]{3,2,1,0:T(8,128)(2,1)S(1)} %pad_maximum_fusion.same, bf16[4,2,528,128]{3,2,1,0:T(8,128)(2,1)S(1)} %collective-permute-done.14.other), custom_call_target="tpu_custom_call" | custom-call | tf_op jit(solution)/shard_map/columns/pallas_call | solution.py:229
  56.5 3.4 %cube.3 = (f32[1024,128]{1,0:T(8,128)S(1)}, bf16[1024,128]{1,0:T(8,128)(2,1)S(1)}, bf16[1024,128]{1,0:T(8,128)(2,1)S(1)}, bf16[1024,128]{1,0:T(8,128)(2,1)S(1)}) custom-call(s32[4]{0:T(128)S(1)} %pad_add_fusion.place_ref, s32[16,128]{1,0:T(8,128)S(1)} %columns.1.scal, bf16[4,2,528,128]{3,2,1,0:T(8,128)(2,1)S(1)} %pad_maximum_fusion.same, ...), custom_call_target="tpu_custom_call" | custom-call | tf_op jit(solution)/shard_map/cube/pallas_call | solution.py:275
  59.9 0.7 collective-permute-start.21
  60.6 3.2 %collective-permute-start.22 = (bf16[1024,128]{1,0:T(8,128)(2,1)S(1)}, bf16[1024,128]{1,0:T(8,128)(2,1)S(1)}, u32[]{:S(2)}, u32[]{:S(2)}) collective-permute-start(bf16[1024,128]{1,0:T(8,128)(2,1)S(1)} %get-tuple-element.37), channel_id=1, source_target_pairs={{0,6},{1,7},{2,4},{3,5},{4,2},{5,3},{6,0},{7,1},{8,14},{9,15},{10,... | collective-permute-start | bytes 786440 | tf_op jit(solution)/shard_map/ppermute | solution.py:29
  63.9 1.7 %collective-permute-start.23 = (bf16[1024,128]{1,0:T(8,128)(2,1)S(1)}, bf16[1024,128]{1,0:T(8,128)(2,1)S(1)}, u32[]{:S(2)}, u32[]{:S(2)}) collective-permute-start(bf16[1024,128]{1,0:T(8,128)(2,1)S(1)} %get-tuple-element.38), channel_id=1, source_target_pairs={{0,4},{1,5},{2,6},{3,7},{4,0},{5,1},{6,2},{7,3},{8,12},{9,13},{10,... | collective-permute-start | bytes 786440 | tf_op jit(solution)/shard_map/ppermute | solution.py:29
  65.6 1.9 %collective-permute-done.16.refs_2_ = bf16[1024,128]{1,0:T(8,128)(2,1)S(1)} collective-permute-done((bf16[1024,128]{1,0:T(8,128)(2,1)S(1)}, bf16[1024,128]{1,0:T(8,128)(2,1)S(1)}, u32[]{:S(2)}, u32[]{:S(2)}) %collective-permute-start.16) | collective-permute-done | bytes 262176 | tf_op jit(solution)/shard_map/ppermute | solution.py:29
  67.5 3.4 %cube.2 = (f32[1024,128]{1,0:T(8,128)S(1)}, bf16[1024,128]{1,0:T(8,128)(2,1)S(1)}, bf16[1024,128]{1,0:T(8,128)(2,1)S(1)}, bf16[1024,128]{1,0:T(8,128)(2,1)S(1)}) custom-call(s32[4]{0:T(128)S(1)} %pad_add_fusion.place_ref, s32[16,128]{1,0:T(8,128)S(1)} %columns.1.scal, bf16[4,2,528,128]{3,2,1,0:T(8,128)(2,1)S(1)} %pad_maximum_fusion.same, ...), custom_call_target="tpu_custom_call" | custom-call | tf_op jit(solution)/shard_map/cube/pallas_call | solution.py:275
  70.9 0.7 collective-permute-start.18
  71.6 3.2 %collective-permute-start.19 = (bf16[1024,128]{1,0:T(8,128)(2,1)S(1)}, bf16[1024,128]{1,0:T(8,128)(2,1)S(1)}, u32[]{:S(2)}, u32[]{:S(2)}) collective-permute-start(bf16[1024,128]{1,0:T(8,128)(2,1)S(1)} %get-tuple-element.33), channel_id=1, source_target_pairs={{0,6},{1,7},{2,4},{3,5},{4,2},{5,3},{6,0},{7,1},{8,14},{9,15},{10,... | collective-permute-start | bytes 786440 | tf_op jit(solution)/shard_map/ppermute | solution.py:29
  74.8 0.6 collective-permute-start.20
  75.4 0.6 collective-permute-done.23.c_ref
  76.0 1.0 %finish.2.refs_0_ = f32[256,1024]{1,0:T(8,128)} custom-call(f32[2,1024,128]{2,1,0:T(8,128)S(1)} %get-tuple-element.24.sq_ref, f32[1024,128]{1,0:T(8,128)S(1)} %get-tuple-element.35.own_ref, bf16[1024,128]{1,0:T(8,128)(2,1)S(1)} %collective-permute-done.21.a_ref, bf16[1024,128]{1,0:T(8,128)(2,1)S(1)} %collective-permute-done.22.b_ref, ...), custom_call_target="tpu_custom_call" | custom-call | tf_op jit(solution)/shard_map/finish/pallas_call | solution.py:300
  77.0 3.1 %collective-permute-done.18.a_ref = bf16[1024,128]{1,0:T(8,128)(2,1)S(1)} collective-permute-done((bf16[1024,128]{1,0:T(8,128)(2,1)S(1)}, bf16[1024,128]{1,0:T(8,128)(2,1)S(1)}, u32[]{:S(2)}, u32[]{:S(2)}) %collective-permute-start.18) | collective-permute-done | bytes 262176 | tf_op jit(solution)/shard_map/ppermute | solution.py:29
  80.1 5.8 %collective-permute-done.19.b_ref = bf16[1024,128]{1,0:T(8,128)(2,1)S(1)} collective-permute-done((bf16[1024,128]{1,0:T(8,128)(2,1)S(1)}, bf16[1024,128]{1,0:T(8,128)(2,1)S(1)}, u32[]{:S(2)}, u32[]{:S(2)}) %collective-permute-start.19) | collective-permute-done | bytes 262176 | tf_op jit(solution)/shard_map/ppermute | solution.py:29
  85.9 1.3 %collective-permute-done.20.c_ref = bf16[1024,128]{1,0:T(8,128)(2,1)S(1)} collective-permute-done((bf16[1024,128]{1,0:T(8,128)(2,1)S(1)}, bf16[1024,128]{1,0:T(8,128)(2,1)S(1)}, u32[]{:S(2)}, u32[]{:S(2)}) %collective-permute-start.20) | collective-permute-done | bytes 262176 | tf_op jit(solution)/shard_map/ppermute | solution.py:29
  87.3 1.0 %finish.3 = f32[256,1024]{1,0:T(8,128)} custom-call(f32[2,1024,128]{2,1,0:T(8,128)S(1)} %get-tuple-element.24.sq_ref, f32[1024,128]{1,0:T(8,128)S(1)} %get-tuple-element.31.own_ref, bf16[1024,128]{1,0:T(8,128)(2,1)S(1)} %collective-permute-done.18.a_ref, bf16[1024,128]{1,0:T(8,128)(2,1)S(1)} %collective-permute-done.19.b_ref, ...), custom_call_target="tpu_custom_call", output_to_operand_aliasing={{}: (5, {})} | custom-call | tf_op jit(solution)/shard_map/finish/pallas_call | solution.py:300
  (13 shorter events, 0.0 us)
Async XLA Ops:
  2.3 9.1 %copy-start = (bf16[2,528,128]{2,1,0:T(8,128)(2,1)S(1)}, bf16[2,528,128]{2,1,0:T(8,128)(2,1)}, u32[]{:S(2)}) copy-start(bf16[2,528,128]{2,1,0:T(8,128)(2,1)} %get-tuple-element.22.refs_0_) | copy-start | bytes 811012
  2.3 16.9 %collective-permute-start = (bf16[2,528,128]{2,1,0:T(8,128)(2,1)}, bf16[2,528,128]{2,1,0:T(8,128)(2,1)S(1)}, u32[]{:S(2)}, u32[]{:S(2)}) collective-permute-start(bf16[2,528,128]{2,1,0:T(8,128)(2,1)} %get-tuple-element.22.refs_0_), channel_id=1, source_target_pairs={{0,32},{1,33},{2,34},{3,35},{4,36},{5,37},{6,38},{7,39},{8,40},{9,... | collective-permute-start | bytes 811016 | tf_op jit(solution)/shard_map/ppermute | solution.py:29
  4.4 26.5 %all-to-all-start = ((bf16[16,144,128]{2,1,0:T(8,128)(2,1)}), bf16[16,144,128]{2,1,0:T(8,128)(2,1)S(1)}, u32[]{:S(2)}, u32[]{:S(2)}) async-start(bf16[16,144,128]{2,1,0:T(8,128)(2,1)} %get-tuple-element.23), calls=%async_computation | async-start | bytes 1179648 | tf_op jit(solution)/shard_map/all_to_all | solution.py:318
  11.5 14.7 %collective-permute-start.1 = (bf16[2,528,128]{2,1,0:T(8,128)(2,1)S(1)}, bf16[2,528,128]{2,1,0:T(8,128)(2,1)S(1)}, u32[]{:S(2)}, u32[]{:S(2)}) collective-permute-start(bf16[2,528,128]{2,1,0:T(8,128)(2,1)S(1)} %copy-done), channel_id=1, source_target_pairs={{0,96},{1,97},{2,98},{3,99},{4,100},{5,101},{6,102},{7,103},{8,104... | collective-permute-start | bytes 811016 | tf_op jit(solution)/shard_map/ppermute | solution.py:29
  14.1 12.1 %collective-permute-start.2 = (bf16[2,528,128]{2,1,0:T(8,128)(2,1)S(1)}, bf16[2,528,128]{2,1,0:T(8,128)(2,1)S(1)}, u32[]{:S(2)}, u32[]{:S(2)}) collective-permute-start(bf16[2,528,128]{2,1,0:T(8,128)(2,1)S(1)} %copy-done), channel_id=1, source_target_pairs={{0,64},{1,65},{2,66},{3,67},{4,68},{5,69},{6,70},{7,71},{8,72},{9,... | collective-permute-start | bytes 811016 | tf_op jit(solution)/shard_map/ppermute | solution.py:29
  15.2 11.5 %collective-permute-start.7 = (bf16[2,528,128]{2,1,0:T(8,128)(2,1)S(1)}, bf16[2,528,128]{2,1,0:T(8,128)(2,1)S(1)}, u32[]{:S(2)}, u32[]{:S(2)}) collective-permute-start(bf16[2,528,128]{2,1,0:T(8,128)(2,1)S(1)} %copy-done), channel_id=1, source_target_pairs={{0,0},{1,1},{2,16},{3,17},{4,32},{5,33},{6,48},{7,49},{8,8},{9,9},... | collective-permute-start | bytes 811016 | tf_op jit(solution)/shard_map/ppermute | solution.py:29
  15.9 11.4 %collective-permute-start.3 = (bf16[2,528,128]{2,1,0:T(8,128)(2,1)S(1)}, bf16[2,528,128]{2,1,0:T(8,128)(2,1)S(1)}, u32[]{:S(2)}, u32[]{:S(2)}) collective-permute-start(bf16[2,528,128]{2,1,0:T(8,128)(2,1)S(1)} %copy-done), channel_id=1, source_target_pairs={{0,16},{1,17},{2,18},{3,19},{4,20},{5,21},{6,22},{7,23},{8,24},{9,... | collective-permute-start | bytes 811016 | tf_op jit(solution)/shard_map/ppermute | solution.py:29
  19.2 10.4 %collective-permute-start.4 = (bf16[2,528,128]{2,1,0:T(8,128)(2,1)S(1)}, bf16[2,528,128]{2,1,0:T(8,128)(2,1)S(1)}, u32[]{:S(2)}, u32[]{:S(2)}) collective-permute-start(bf16[2,528,128]{2,1,0:T(8,128)(2,1)S(1)} %collective-permute-done.refs_1_), channel_id=1, source_target_pairs={{0,16},{1,17},{2,18},{3,19},{4,20},{5,21},{6,22},{7,23},{8,24},{9,... | collective-permute-start | bytes 811016 | tf_op jit(solution)/shard_map/ppermute | solution.py:29
  26.2 4.7 %collective-permute-start.5 = (bf16[2,528,128]{2,1,0:T(8,128)(2,1)S(1)}, bf16[2,528,128]{2,1,0:T(8,128)(2,1)S(1)}, u32[]{:S(2)}, u32[]{:S(2)}) collective-permute-start(bf16[2,528,128]{2,1,0:T(8,128)(2,1)S(1)} %collective-permute-done.1.refs_2_), channel_id=1, source_target_pairs={{0,16},{1,17},{2,18},{3,19},{4,20},{5,21},{6,22},{7,23},{8,24},{9,... | collective-permute-start | bytes 811016 | tf_op jit(solution)/shard_map/ppermute | solution.py:29
  26.2 4.7 %collective-permute-start.6 = (bf16[2,528,128]{2,1,0:T(8,128)(2,1)S(1)}, bf16[2,528,128]{2,1,0:T(8,128)(2,1)S(1)}, u32[]{:S(2)}, u32[]{:S(2)}) collective-permute-start(bf16[2,528,128]{2,1,0:T(8,128)(2,1)S(1)} %collective-permute-done.2.refs_3_), channel_id=1, source_target_pairs={{0,16},{1,17},{2,18},{3,19},{4,20},{5,21},{6,22},{7,23},{8,24},{9,... | collective-permute-start | bytes 811016 | tf_op jit(solution)/shard_map/ppermute | solution.py:29
  26.7 11.4 %collective-permute-start.8 = (bf16[2,528,128]{2,1,0:T(8,128)(2,1)S(1)}, bf16[2,528,128]{2,1,0:T(8,128)(2,1)S(1)}, u32[]{:S(2)}, u32[]{:S(2)}) collective-permute-start(bf16[2,528,128]{2,1,0:T(8,128)(2,1)S(1)} %collective-permute-done.7), channel_id=1, source_target_pairs={{0,32},{1,33},{2,34},{3,35},{4,36},{5,37},{6,38},{7,39},{8,40},{9,... | collective-permute-start | bytes 811016 | tf_op jit(solution)/shard_map/ppermute | solution.py:29
  27.3 14.5 %collective-permute-start.9 = (bf16[2,528,128]{2,1,0:T(8,128)(2,1)S(1)}, bf16[2,528,128]{2,1,0:T(8,128)(2,1)}, u32[]{:S(2)}, u32[]{:S(2)}) collective-permute-start(bf16[2,528,128]{2,1,0:T(8,128)(2,1)S(1)} %collective-permute-done.7), channel_id=1, source_target_pairs={{0,96},{1,97},{2,98},{3,99},{4,100},{5,101},{6,102},{7,103},{8,104... | collective-permute-start | bytes 811016 | tf_op jit(solution)/shard_map/ppermute | solution.py:29
  29.7 13.7 %collective-permute-start.10 = (bf16[2,528,128]{2,1,0:T(8,128)(2,1)S(1)}, bf16[2,528,128]{2,1,0:T(8,128)(2,1)}, u32[]{:S(2)}, u32[]{:S(2)}) collective-permute-start(bf16[2,528,128]{2,1,0:T(8,128)(2,1)S(1)} %collective-permute-done.7), channel_id=1, source_target_pairs={{0,64},{1,65},{2,66},{3,67},{4,68},{5,69},{6,70},{7,71},{8,72},{9,... | collective-permute-start | bytes 811016 | tf_op jit(solution)/shard_map/ppermute | solution.py:29
  34.4 10.1 %collective-permute-start.11 = (bf16[1024,128]{1,0:T(8,128)(2,1)S(1)}, bf16[1024,128]{1,0:T(8,128)(2,1)S(1)}, u32[]{:S(2)}, u32[]{:S(2)}) collective-permute-start(bf16[1024,128]{1,0:T(8,128)(2,1)S(1)} %get-tuple-element.25.refs_0_), channel_id=1, source_target_pairs={{0,8},{1,9},{2,10},{3,11},{4,12},{5,13},{6,14},{7,15},{8,0},{9,1},... | collective-permute-start | bytes 786440 | tf_op jit(solution)/shard_map/ppermute | solution.py:29
  36.1 15.5 %collective-permute-start.12 = (bf16[1024,128]{1,0:T(8,128)(2,1)S(1)}, bf16[1024,128]{1,0:T(8,128)(2,1)S(1)}, u32[]{:S(2)}, u32[]{:S(2)}) collective-permute-start(bf16[1024,128]{1,0:T(8,128)(2,1)S(1)} %get-tuple-element.25.refs_0_), channel_id=1, source_target_pairs={{0,9},{1,8},{2,11},{3,10},{4,13},{5,12},{6,15},{7,14},{8,1},{9,0},... | collective-permute-start | bytes 786440 | tf_op jit(solution)/shard_map/ppermute | solution.py:29
  38.1 13.5 %collective-permute-start.13 = (bf16[1024,128]{1,0:T(8,128)(2,1)S(1)}, bf16[1024,128]{1,0:T(8,128)(2,1)S(1)}, u32[]{:S(2)}, u32[]{:S(2)}) collective-permute-start(bf16[1024,128]{1,0:T(8,128)(2,1)S(1)} %get-tuple-element.25.refs_0_), channel_id=1, source_target_pairs={{0,1},{1,0},{2,3},{3,2},{4,5},{5,4},{6,7},{7,6},{8,9},{9,8},{10,11... | collective-permute-start | bytes 786440 | tf_op jit(solution)/shard_map/ppermute | solution.py:29
  51.6 3.5 %collective-permute-start.14 = (bf16[4,2,528,128]{3,2,1,0:T(8,128)(2,1)S(1)}, bf16[4,2,528,128]{3,2,1,0:T(8,128)(2,1)S(1)}, u32[]{:S(2)}, u32[]{:S(2)}) collective-permute-start(bf16[4,2,528,128]{3,2,1,0:T(8,128)(2,1)S(1)} %pad_maximum_fusion.same), channel_id=1, source_target_pairs={{0,16},{1,17},{2,18},{3,19},{4,20},{5,21},{6,22},{7,23},{8,24},{9,... | collective-permute-start | bytes 3244040 | tf_op jit(solution)/shard_map/ppermute | solution.py:29
  51.6 12.3 %collective-permute-start.17 = (bf16[1024,128]{1,0:T(8,128)(2,1)S(1)}, bf16[1024,128]{1,0:T(8,128)(2,1)S(1)}, u32[]{:S(2)}, u32[]{:S(2)}) collective-permute-start(bf16[1024,128]{1,0:T(8,128)(2,1)S(1)} %get-tuple-element.30.refs_0_), channel_id=1, source_target_pairs={{0,1},{1,0},{2,3},{3,2},{4,5},{5,4},{6,7},{7,6},{8,9},{9,8},{10,11... | collective-permute-start | bytes 786440 | tf_op jit(solution)/shard_map/ppermute | solution.py:29
  52.9 14.5 %collective-permute-start.16 = (bf16[1024,128]{1,0:T(8,128)(2,1)S(1)}, bf16[1024,128]{1,0:T(8,128)(2,1)S(1)}, u32[]{:S(2)}, u32[]{:S(2)}) collective-permute-start(bf16[1024,128]{1,0:T(8,128)(2,1)S(1)} %get-tuple-element.30.refs_0_), channel_id=1, source_target_pairs={{0,9},{1,8},{2,11},{3,10},{4,13},{5,12},{6,15},{7,14},{8,1},{9,0},... | collective-permute-start | bytes 786440 | tf_op jit(solution)/shard_map/ppermute | solution.py:29
  54.0 13.4 %collective-permute-start.15 = (bf16[1024,128]{1,0:T(8,128)(2,1)S(1)}, bf16[1024,128]{1,0:T(8,128)(2,1)S(1)}, u32[]{:S(2)}, u32[]{:S(2)}) collective-permute-start(bf16[1024,128]{1,0:T(8,128)(2,1)S(1)} %get-tuple-element.30.refs_0_), channel_id=1, source_target_pairs={{0,8},{1,9},{2,10},{3,11},{4,12},{5,13},{6,14},{7,15},{8,0},{9,1},... | collective-permute-start | bytes 786440 | tf_op jit(solution)/shard_map/ppermute | solution.py:29
  59.9 14.9 %collective-permute-start.21 = (bf16[1024,128]{1,0:T(8,128)(2,1)S(1)}, bf16[1024,128]{1,0:T(8,128)(2,1)S(1)}, u32[]{:S(2)}, u32[]{:S(2)}) collective-permute-start(bf16[1024,128]{1,0:T(8,128)(2,1)S(1)} %get-tuple-element.36), channel_id=1, source_target_pairs={{0,2},{1,3},{2,0},{3,1},{4,6},{5,7},{6,4},{7,5},{8,10},{9,11},{10,... | collective-permute-start | bytes 786440 | tf_op jit(solution)/shard_map/ppermute | solution.py:29
  60.6 14.8 %collective-permute-start.22 = (bf16[1024,128]{1,0:T(8,128)(2,1)S(1)}, bf16[1024,128]{1,0:T(8,128)(2,1)S(1)}, u32[]{:S(2)}, u32[]{:S(2)}) collective-permute-start(bf16[1024,128]{1,0:T(8,128)(2,1)S(1)} %get-tuple-element.37), channel_id=1, source_target_pairs={{0,6},{1,7},{2,4},{3,5},{4,2},{5,3},{6,0},{7,1},{8,14},{9,15},{10,... | collective-permute-start | bytes 786440 | tf_op jit(solution)/shard_map/ppermute | solution.py:29
  63.9 12.1 %collective-permute-start.23 = (bf16[1024,128]{1,0:T(8,128)(2,1)S(1)}, bf16[1024,128]{1,0:T(8,128)(2,1)S(1)}, u32[]{:S(2)}, u32[]{:S(2)}) collective-permute-start(bf16[1024,128]{1,0:T(8,128)(2,1)S(1)} %get-tuple-element.38), channel_id=1, source_target_pairs={{0,4},{1,5},{2,6},{3,7},{4,0},{5,1},{6,2},{7,3},{8,12},{9,13},{10,... | collective-permute-start | bytes 786440 | tf_op jit(solution)/shard_map/ppermute | solution.py:29
  70.9 9.2 %collective-permute-start.18 = (bf16[1024,128]{1,0:T(8,128)(2,1)S(1)}, bf16[1024,128]{1,0:T(8,128)(2,1)S(1)}, u32[]{:S(2)}, u32[]{:S(2)}) collective-permute-start(bf16[1024,128]{1,0:T(8,128)(2,1)S(1)} %get-tuple-element.32), channel_id=1, source_target_pairs={{0,2},{1,3},{2,0},{3,1},{4,6},{5,7},{6,4},{7,5},{8,10},{9,11},{10,... | collective-permute-start | bytes 786440 | tf_op jit(solution)/shard_map/ppermute | solution.py:29
  71.6 14.4 %collective-permute-start.19 = (bf16[1024,128]{1,0:T(8,128)(2,1)S(1)}, bf16[1024,128]{1,0:T(8,128)(2,1)S(1)}, u32[]{:S(2)}, u32[]{:S(2)}) collective-permute-start(bf16[1024,128]{1,0:T(8,128)(2,1)S(1)} %get-tuple-element.33), channel_id=1, source_target_pairs={{0,6},{1,7},{2,4},{3,5},{4,2},{5,3},{6,0},{7,1},{8,14},{9,15},{10,... | collective-permute-start | bytes 786440 | tf_op jit(solution)/shard_map/ppermute | solution.py:29
  74.8 12.4 %collective-permute-start.20 = (bf16[1024,128]{1,0:T(8,128)(2,1)S(1)}, bf16[1024,128]{1,0:T(8,128)(2,1)S(1)}, u32[]{:S(2)}, u32[]{:S(2)}) collective-permute-start(bf16[1024,128]{1,0:T(8,128)(2,1)S(1)} %get-tuple-element.34), channel_id=1, source_target_pairs={{0,4},{1,5},{2,6},{3,7},{4,0},{5,1},{6,2},{7,3},{8,12},{9,13},{10,... | collective-permute-start | bytes 786440 | tf_op jit(solution)/shard_map/ppermute | solution.py:29

commit v4 on v3

--- a/solution.py
+++ b/solution.py
@@ -215,29 +215,28 @@
     )(where, *ring, *other, slab)
 
 
-def columns_kernel(same, other, scal, ints, sem):
-    for b, ref in enumerate((same, other)):
-        for n in range(8):
-            row = ref[n // 2, n % 2, 512:528, :].astype(F32)[0:1, :]
-            ints[8 * b + n : 8 * b + n + 1, :] = row.astype(I32)
+def columns_kernel(part, scal, ints, sem):
+    for n in range(8):
+        row = part[n // 2, n % 2, 512:528, :].astype(F32)[0:1, :]
+        ints[n : n + 1, :] = row.astype(I32)
     to_scal = pltpu.make_async_copy(ints, scal, sem)
     to_scal.start()
     to_scal.wait()
 
 
-def columns_of(same, other):
+def columns_of(part):
     return pl.pallas_call(
         columns_kernel,
-        out_shape=jax.ShapeDtypeStruct((16, 128), I32),
-        in_specs=[VMEM, VMEM],
+        out_shape=jax.ShapeDtypeStruct((8, 128), I32),
+        in_specs=[VMEM],
         out_specs=SMEM,
-        scratch_shapes=[pltpu.VMEM((16, 128), I32), pltpu.SemaphoreType.DMA],
+        scratch_shapes=[pltpu.VMEM((8, 128), I32), pltpu.SemaphoreType.DMA],
         compiler_params=PARAMS,
         name="columns",
-    )(same, other)
-
-
-def cube_kernel(place_ref, scal, same, other, *refs):
+    )(part)
+
+
+def cube_kernel(place_ref, scal_same, scal_other, same, other, *refs):
     squares, outs, (acc,) = refs[:4], refs[4:8], refs[8:]
     z, core, x, y = (place_ref[n] for n in range(4))
     acc[...] = jnp.zeros_like(acc)
@@ -251,7 +250,7 @@
         def step(quad, carry, n=n, source=source, half=half):
             right = squares[n][pl.ds(pl.multiple_of(quad * 256, 256), 256), :]
             rows = pl.ds(pl.multiple_of(quad * 128, 128), 128)
-            for b, panel in enumerate((same, other)):
+            for b, (panel, scal) in enumerate(((same, scal_same), (other, scal_other))):
                 for m in range(2):
                     there = 2 * m + (core ^ b)
                     flip = z ^ (2 * lax.rem(source, 2) + m)
@@ -261,7 +260,7 @@
                     left = jnp.concatenate([t * mask for mask in masks], axis=0)
                     out = jnp.dot(left, right, preferred_element_type=F32)
                     for c4 in range(4):
-                        j = lax.rem(scal[8 * b + 2 * at + half, quad * 4 + c4], 16)
+                        j = lax.rem(scal[2 * at + half, quad * 4 + c4], 16)
                         into = pl.ds(pl.multiple_of(j * 64, 64), 64)
                         acc[there, into, :] += out[c4 * 64 : c4 * 64 + 64, :]
             return carry
@@ -278,12 +277,12 @@
             jax.ShapeDtypeStruct((1024, 128), F32),
             *[jax.ShapeDtypeStruct((1024, 128), BF16)] * 3,
         ),
-        in_specs=[SMEM, SMEM] + [VMEM] * 6,
+        in_specs=[SMEM] * 3 + [VMEM] * 6,
         out_specs=(VMEM,) * 4,
         scratch_shapes=[pltpu.VMEM((4, 1024, 128), F32)],
         compiler_params=PARAMS,
         name="cube",
-    )(where, columns, same, other, *squares)
+    )(where, *columns, same, other, *squares)
 
 
 def finish_kernel(h, sq_ref, own_ref, a_ref, b_ref, c_ref, *refs):
@@ -325,7 +324,7 @@
         if turned_other is None:
             turned = jnp.stack(turned_ring)
             turned_other = swap(after(turned, *moved), core=1)
-            columns = columns_of(turned, turned_other)
+            columns = [columns_of(turned), columns_of(turned_other)]
         own, *outs = cube_of(where, columns, turned, turned_other, [mine, *moved])
         moved = [(v,) for v in moved]
         outs = [swap(v, y=d) for v, d in zip(outs, FLIPS[1:])]

time: 88.6 us -> 89.6 us (1.011)
  Pallas kernels: 16 us -> 17.2 us
  starting transfers between devices: 40.1 us -> 39 us
  waiting for transfers between devices: 30.9 us -> 31.8 us
    pallas_call x1 -> x2, Pallas kernels: 1.4 us -> 2.53 us  [columns_of(): pl.pallas_call(columns_kernel, out_shape=jax.ShapeDtypeStruct((8, 128), I...]
    ppermute x24, starting transfers between devices: 33 us -> 32 us  [permute(): return lax.ppermute(value, AXES, pairs)]
    ppermute x24, waiting for transfers between devices: 30.9 us -> 31.8 us  [permute(): return lax.ppermute(value, AXES, pairs)]
  transfers between devices with their start and end apart: 25 -> 25, of which waited for: 9 -> 10; matrix products, arithmetic and copies ran while one was open for 1% -> 1% of each run, Pallas kernels for 14% -> 15%
where the time goes in v4:
time: 89.6 us; the launch traced here: 89.4 us
  starting transfers between devices  39 us (44%)
  waiting for transfers between devices  31.8 us (35%)
  Pallas kernels  17.2 us (19%)
  other arithmetic  1.25 us (1%)
    ppermute x24, starting transfers between devices, permute(): return lax.ppermute(value, AXES, pairs)  32 us
    ppermute x24, waiting for transfers between devices, permute(): return lax.ppermute(value, AXES, pairs)  31.8 us
    all_to_all x1, starting transfers between devices, body(): slab = lax.all_to_all(slab, ('col', 'depth'), 0, 0, tiled=True)  7.03 us
    pallas_call x2, Pallas kernels, cube_of(): pl.pallas_call(cube_kernel, out_shape=(jax.ShapeDtypeStruct((1024, 128),...  6.86 us
    pallas_call x1, Pallas kernels, square_of(): pl.pallas_call(square_kernel, out_shape=(jax.ShapeDtypeStruct((2, 1024, 1...  3.41 us
    pallas_call x2, Pallas kernels, columns_of(): pl.pallas_call(columns_kernel, out_shape=jax.ShapeDtypeStruct((8, 128), I...  2.53 us
    pallas_call x1, Pallas kernels, pack(): pl.pallas_call(pack_kernel, out_shape=(jax.ShapeDtypeStruct((2, HALF, 128...  2.31 us
    pallas_call x2, Pallas kernels, finish(): pl.pallas_call(functools.partial(finish_kernel, h), out_shape=jax.ShapeDt...  2.04 us
  transfers between devices with their start and end apart: 25, of which 10 were waited for; matrix products, arithmetic and copies ran while one was open for 1% of the time, Pallas kernels for 15%

profile of v4, /device:TPU:0, one launch (start us, length us, event | category | flops | bytes accessed | tf_op | source)
XLA Modules:
  0.0 89.4 jit_solution(13159524729503721174)
XLA Ops:
  0.0 2.3 %pack.1 = (bf16[2,528,128]{2,1,0:T(8,128)(2,1)}, bf16[16,144,128]{2,1,0:T(8,128)(2,1)}) custom-call(bf16[32,4096]{1,0:T(8,128)(2,1)} %bitcast.12, s32[1,32]{1,0:T(1,128)} %bitcast.13), custom_call_target="tpu_custom_call" | custom-call | tf_op jit(solution)/shard_map/pack/pallas_call | solution.py:109
  2.3 2.1 %collective-permute-start = (bf16[2,528,128]{2,1,0:T(8,128)(2,1)}, bf16[2,528,128]{2,1,0:T(8,128)(2,1)S(1)}, u32[]{:S(2)}, u32[]{:S(2)}) collective-permute-start(bf16[2,528,128]{2,1,0:T(8,128)(2,1)} %get-tuple-element.22.refs_0_), channel_id=1, source_target_pairs={{0,32},{1,33},{2,34},{3,35},{4,36},{5,37},{6,38},{7,39},{8,40},{9,... | collective-permute-start | bytes 811016 | tf_op jit(solution)/shard_map/ppermute | solution.py:29
  4.4 7.0 %all-to-all-start = ((bf16[16,144,128]{2,1,0:T(8,128)(2,1)}), bf16[16,144,128]{2,1,0:T(8,128)(2,1)S(1)}, u32[]{:S(2)}, u32[]{:S(2)}) async-start(bf16[16,144,128]{2,1,0:T(8,128)(2,1)} %get-tuple-element.23), calls=%async_computation | async-start | bytes 1179648 | tf_op jit(solution)/shard_map/all_to_all | solution.py:317
  11.5 2.6 %collective-permute-start.1 = (bf16[2,528,128]{2,1,0:T(8,128)(2,1)S(1)}, bf16[2,528,128]{2,1,0:T(8,128)(2,1)S(1)}, u32[]{:S(2)}, u32[]{:S(2)}) collective-permute-start(bf16[2,528,128]{2,1,0:T(8,128)(2,1)S(1)} %copy-done), channel_id=1, source_target_pairs={{0,96},{1,97},{2,98},{3,99},{4,100},{5,101},{6,102},{7,103},{8,104... | collective-permute-start | bytes 811016 | tf_op jit(solution)/shard_map/ppermute | solution.py:29
  14.1 1.2 %collective-permute-start.2 = (bf16[2,528,128]{2,1,0:T(8,128)(2,1)S(1)}, bf16[2,528,128]{2,1,0:T(8,128)(2,1)S(1)}, u32[]{:S(2)}, u32[]{:S(2)}) collective-permute-start(bf16[2,528,128]{2,1,0:T(8,128)(2,1)S(1)} %copy-done), channel_id=1, source_target_pairs={{0,64},{1,65},{2,66},{3,67},{4,68},{5,69},{6,70},{7,71},{8,72},{9,... | collective-permute-start | bytes 811016 | tf_op jit(solution)/shard_map/ppermute | solution.py:29
  15.2 0.7 collective-permute-start.7
  15.9 3.3 %collective-permute-start.3 = (bf16[2,528,128]{2,1,0:T(8,128)(2,1)S(1)}, bf16[2,528,128]{2,1,0:T(8,128)(2,1)S(1)}, u32[]{:S(2)}, u32[]{:S(2)}) collective-permute-start(bf16[2,528,128]{2,1,0:T(8,128)(2,1)S(1)} %copy-done), channel_id=1, source_target_pairs={{0,16},{1,17},{2,18},{3,19},{4,20},{5,21},{6,22},{7,23},{8,24},{9,... | collective-permute-start | bytes 811016 | tf_op jit(solution)/shard_map/ppermute | solution.py:29
  19.2 0.0 collective-permute-done.refs_1_
  19.2 0.1 collective-permute-start.4
  19.3 6.9 %collective-permute-done.1.refs_2_ = bf16[2,528,128]{2,1,0:T(8,128)(2,1)S(1)} collective-permute-done((bf16[2,528,128]{2,1,0:T(8,128)(2,1)S(1)}, bf16[2,528,128]{2,1,0:T(8,128)(2,1)S(1)}, u32[]{:S(2)}, u32[]{:S(2)}) %collective-permute-start.1) | collective-permute-done | bytes 270368 | tf_op jit(solution)/shard_map/ppermute | solution.py:29
  26.2 0.0 collective-permute-start.5
  26.2 0.5 collective-permute-start.6
  26.7 0.6 collective-permute-start.8
  27.3 2.3 %collective-permute-start.9 = (bf16[2,528,128]{2,1,0:T(8,128)(2,1)S(1)}, bf16[2,528,128]{2,1,0:T(8,128)(2,1)}, u32[]{:S(2)}, u32[]{:S(2)}) collective-permute-start(bf16[2,528,128]{2,1,0:T(8,128)(2,1)S(1)} %collective-permute-done.7), channel_id=1, source_target_pairs={{0,96},{1,97},{2,98},{3,99},{4,100},{5,101},{6,102},{7,103},{8,104... | collective-permute-start | bytes 811016 | tf_op jit(solution)/shard_map/ppermute | solution.py:29
  29.7 1.2 %collective-permute-start.10 = (bf16[2,528,128]{2,1,0:T(8,128)(2,1)S(1)}, bf16[2,528,128]{2,1,0:T(8,128)(2,1)}, u32[]{:S(2)}, u32[]{:S(2)}) collective-permute-start(bf16[2,528,128]{2,1,0:T(8,128)(2,1)S(1)} %collective-permute-done.7), channel_id=1, source_target_pairs={{0,64},{1,65},{2,66},{3,67},{4,68},{5,69},{6,70},{7,71},{8,72},{9,... | collective-permute-start | bytes 811016 | tf_op jit(solution)/shard_map/ppermute | solution.py:29
  30.9 0.1 pad_add_fusion.place_ref
  30.9 3.4 %square.1 = (f32[2,1024,128]{2,1,0:T(8,128)S(1)}, bf16[1024,128]{1,0:T(8,128)(2,1)S(1)}, bf16[1024,128]{1,0:T(8,128)(2,1)S(1)}) custom-call(s32[4]{0:T(128)S(1)} %pad_add_fusion.place_ref, bf16[2,528,128]{2,1,0:T(8,128)(2,1)S(1)} %copy-done, bf16[2,528,128]{2,1,0:T(8,128)(2,1)S(1)} %collective-permute-done.refs_1_, ...), custom_call_target="tpu_custom_call" | custom-call | tf_op jit(solution)/shard_map/square/pallas_call | solution.py:198
  34.4 1.7 %collective-permute-start.11 = (bf16[1024,128]{1,0:T(8,128)(2,1)S(1)}, bf16[1024,128]{1,0:T(8,128)(2,1)S(1)}, u32[]{:S(2)}, u32[]{:S(2)}) collective-permute-start(bf16[1024,128]{1,0:T(8,128)(2,1)S(1)} %get-tuple-element.25.refs_0_), channel_id=1, source_target_pairs={{0,8},{1,9},{2,10},{3,11},{4,12},{5,13},{6,14},{7,15},{8,0},{9,1},... | collective-permute-start | bytes 786440 | tf_op jit(solution)/shard_map/ppermute | solution.py:29
  36.1 2.1 %collective-permute-start.12 = (bf16[1024,128]{1,0:T(8,128)(2,1)S(1)}, bf16[1024,128]{1,0:T(8,128)(2,1)S(1)}, u32[]{:S(2)}, u32[]{:S(2)}) collective-permute-start(bf16[1024,128]{1,0:T(8,128)(2,1)S(1)} %get-tuple-element.25.refs_0_), channel_id=1, source_target_pairs={{0,9},{1,8},{2,11},{3,10},{4,13},{5,12},{6,15},{7,14},{8,1},{9,0},... | collective-permute-start | bytes 786440 | tf_op jit(solution)/shard_map/ppermute | solution.py:29
  38.1 1.1 %collective-permute-start.13 = (bf16[1024,128]{1,0:T(8,128)(2,1)S(1)}, bf16[1024,128]{1,0:T(8,128)(2,1)S(1)}, u32[]{:S(2)}, u32[]{:S(2)}) collective-permute-start(bf16[1024,128]{1,0:T(8,128)(2,1)S(1)} %get-tuple-element.25.refs_0_), channel_id=1, source_target_pairs={{0,1},{1,0},{2,3},{3,2},{4,5},{5,4},{6,7},{7,6},{8,9},{9,8},{10,11... | collective-permute-start | bytes 786440 | tf_op jit(solution)/shard_map/ppermute | solution.py:29
  39.2 2.7 %collective-permute-done.9 = bf16[2,528,128]{2,1,0:T(8,128)(2,1)} collective-permute-done((bf16[2,528,128]{2,1,0:T(8,128)(2,1)S(1)}, bf16[2,528,128]{2,1,0:T(8,128)(2,1)}, u32[]{:S(2)}, u32[]{:S(2)}) %collective-permute-start.9) | collective-permute-done | bytes 270368 | tf_op jit(solution)/shard_map/ppermute | solution.py:29
  41.9 1.5 %collective-permute-done.10 = bf16[2,528,128]{2,1,0:T(8,128)(2,1)} collective-permute-done((bf16[2,528,128]{2,1,0:T(8,128)(2,1)S(1)}, bf16[2,528,128]{2,1,0:T(8,128)(2,1)}, u32[]{:S(2)}, u32[]{:S(2)}) %collective-permute-start.10) | collective-permute-done | bytes 270368 | tf_op jit(solution)/shard_map/ppermute | solution.py:29
  43.3 1.2 %pad_maximum_fusion.part.same = bf16[4,2,528,128]{3,2,1,0:T(8,128)(2,1)S(1)} fusion(bf16[1,2,528,128]{3,2,1,0:T(8,128)(2,1)} %bitcast.9, bf16[1,2,528,128]{3,2,1,0:T(8,128)(2,1)} %bitcast.8, bf16[1,2,528,128]{3,2,1,0:T(8,128)(2,1)S(1)} %bitcast.11, bf16[1,2,528,128]{3,2,1,0:T(8,128)(2,1)S(1)} %bitcast.10), kind=kLoop, calls=%fused_computation | loop fusion | flops 1622016 | bytes 2162688 | tf_op jit(solution)/shard_map/stack | solution.py:325
  44.5 0.0 collective-permute-done.11.refs_1_
  44.5 7.1 %collective-permute-done.12.refs_2_ = bf16[1024,128]{1,0:T(8,128)(2,1)S(1)} collective-permute-done((bf16[1024,128]{1,0:T(8,128)(2,1)S(1)}, bf16[1024,128]{1,0:T(8,128)(2,1)S(1)}, u32[]{:S(2)}, u32[]{:S(2)}) %collective-permute-start.12) | collective-permute-done | bytes 262176 | tf_op jit(solution)/shard_map/ppermute | solution.py:29
  51.6 0.0 collective-permute-done.13.refs_3_
  51.6 1.3 %collective-permute-start.17 = (bf16[1024,128]{1,0:T(8,128)(2,1)S(1)}, bf16[1024,128]{1,0:T(8,128)(2,1)S(1)}, u32[]{:S(2)}, u32[]{:S(2)}) collective-permute-start(bf16[1024,128]{1,0:T(8,128)(2,1)S(1)} %get-tuple-element.30.refs_0_), channel_id=1, source_target_pairs={{0,1},{1,0},{2,3},{3,2},{4,5},{5,4},{6,7},{7,6},{8,9},{9,8},{10,11... | collective-permute-start | bytes 786440 | tf_op jit(solution)/shard_map/ppermute | solution.py:29
  52.9 1.1 %collective-permute-start.16 = (bf16[1024,128]{1,0:T(8,128)(2,1)S(1)}, bf16[1024,128]{1,0:T(8,128)(2,1)S(1)}, u32[]{:S(2)}, u32[]{:S(2)}) collective-permute-start(bf16[1024,128]{1,0:T(8,128)(2,1)S(1)} %get-tuple-element.30.refs_0_), channel_id=1, source_target_pairs={{0,9},{1,8},{2,11},{3,10},{4,13},{5,12},{6,15},{7,14},{8,1},{9,0},... | collective-permute-start | bytes 786440 | tf_op jit(solution)/shard_map/ppermute | solution.py:29
  54.0 1.1 %collective-permute-start.15 = (bf16[1024,128]{1,0:T(8,128)(2,1)S(1)}, bf16[1024,128]{1,0:T(8,128)(2,1)S(1)}, u32[]{:S(2)}, u32[]{:S(2)}) collective-permute-start(bf16[1024,128]{1,0:T(8,128)(2,1)S(1)} %get-tuple-element.30.refs_0_), channel_id=1, source_target_pairs={{0,8},{1,9},{2,10},{3,11},{4,12},{5,13},{6,14},{7,15},{8,0},{9,1},... | collective-permute-start | bytes 786440 | tf_op jit(solution)/shard_map/ppermute | solution.py:29
  55.1 1.3 %columns.2.scal_same = s32[8,128]{1,0:T(8,128)S(1)} custom-call(bf16[4,2,528,128]{3,2,1,0:T(8,128)(2,1)S(1)} %pad_maximum_fusion.part.same), custom_call_target="tpu_custom_call" | custom-call | tf_op jit(solution)/shard_map/columns/pallas_call | solution.py:228
  56.4 1.3 %columns.3.scal_other = s32[8,128]{1,0:T(8,128)S(1)} custom-call(bf16[4,2,528,128]{3,2,1,0:T(8,128)(2,1)S(1)} %collective-permute-done.14.part.other), custom_call_target="tpu_custom_call" | custom-call | tf_op jit(solution)/shard_map/columns/pallas_call | solution.py:228
  57.7 3.4 %cube.3 = (f32[1024,128]{1,0:T(8,128)S(1)}, bf16[1024,128]{1,0:T(8,128)(2,1)S(1)}, bf16[1024,128]{1,0:T(8,128)(2,1)S(1)}, bf16[1024,128]{1,0:T(8,128)(2,1)S(1)}) custom-call(s32[4]{0:T(128)S(1)} %pad_add_fusion.place_ref, s32[8,128]{1,0:T(8,128)S(1)} %columns.2.scal_same, s32[8,128]{1,0:T(8,128)S(1)} %columns.3.scal_other, ...), custom_call_target="tpu_custom_call" | custom-call | tf_op jit(solution)/shard_map/cube/pallas_call | solution.py:274
  61.1 0.7 collective-permute-start.21
  61.8 3.2 %collective-permute-start.22 = (bf16[1024,128]{1,0:T(8,128)(2,1)S(1)}, bf16[1024,128]{1,0:T(8,128)(2,1)S(1)}, u32[]{:S(2)}, u32[]{:S(2)}) collective-permute-start(bf16[1024,128]{1,0:T(8,128)(2,1)S(1)} %get-tuple-element.37), channel_id=1, source_target_pairs={{0,6},{1,7},{2,4},{3,5},{4,2},{5,3},{6,0},{7,1},{8,14},{9,15},{10,... | collective-permute-start | bytes 786440 | tf_op jit(solution)/shard_map/ppermute | solution.py:29
  65.0 0.6 collective-permute-start.23
  65.7 1.8 %collective-permute-done.16.refs_2_ = bf16[1024,128]{1,0:T(8,128)(2,1)S(1)} collective-permute-done((bf16[1024,128]{1,0:T(8,128)(2,1)S(1)}, bf16[1024,128]{1,0:T(8,128)(2,1)S(1)}, u32[]{:S(2)}, u32[]{:S(2)}) %collective-permute-start.16) | collective-permute-done | bytes 262176 | tf_op jit(solution)/shard_map/ppermute | solution.py:29
  67.5 0.0 collective-permute-done.15.refs_1_
  67.5 3.4 %cube.2 = (f32[1024,128]{1,0:T(8,128)S(1)}, bf16[1024,128]{1,0:T(8,128)(2,1)S(1)}, bf16[1024,128]{1,0:T(8,128)(2,1)S(1)}, bf16[1024,128]{1,0:T(8,128)(2,1)S(1)}) custom-call(s32[4]{0:T(128)S(1)} %pad_add_fusion.place_ref, s32[8,128]{1,0:T(8,128)S(1)} %columns.2.scal_same, s32[8,128]{1,0:T(8,128)S(1)} %columns.3.scal_other, ...), custom_call_target="tpu_custom_call" | custom-call | tf_op jit(solution)/shard_map/cube/pallas_call | solution.py:274
  70.9 0.7 collective-permute-start.18
  71.6 3.2 %collective-permute-start.19 = (bf16[1024,128]{1,0:T(8,128)(2,1)S(1)}, bf16[1024,128]{1,0:T(8,128)(2,1)S(1)}, u32[]{:S(2)}, u32[]{:S(2)}) collective-permute-start(bf16[1024,128]{1,0:T(8,128)(2,1)S(1)} %get-tuple-element.33), channel_id=1, source_target_pairs={{0,6},{1,7},{2,4},{3,5},{4,2},{5,3},{6,0},{7,1},{8,14},{9,15},{10,... | collective-permute-start | bytes 786440 | tf_op jit(solution)/shard_map/ppermute | solution.py:29
  74.8 0.6 collective-permute-start.20
  75.4 1.3 %collective-permute-done.22.b_ref = bf16[1024,128]{1,0:T(8,128)(2,1)S(1)} collective-permute-done((bf16[1024,128]{1,0:T(8,128)(2,1)S(1)}, bf16[1024,128]{1,0:T(8,128)(2,1)S(1)}, u32[]{:S(2)}, u32[]{:S(2)}) %collective-permute-start.22) | collective-permute-done | bytes 262176 | tf_op jit(solution)/shard_map/ppermute | solution.py:29
  76.7 1.4 %collective-permute-done.23.c_ref = bf16[1024,128]{1,0:T(8,128)(2,1)S(1)} collective-permute-done((bf16[1024,128]{1,0:T(8,128)(2,1)S(1)}, bf16[1024,128]{1,0:T(8,128)(2,1)S(1)}, u32[]{:S(2)}, u32[]{:S(2)}) %collective-permute-start.23) | collective-permute-done | bytes 262176 | tf_op jit(solution)/shard_map/ppermute | solution.py:29
  78.1 1.0 %finish.2.refs_0_ = f32[256,1024]{1,0:T(8,128)} custom-call(f32[2,1024,128]{2,1,0:T(8,128)S(1)} %get-tuple-element.24.sq_ref, f32[1024,128]{1,0:T(8,128)S(1)} %get-tuple-element.35.own_ref, bf16[1024,128]{1,0:T(8,128)(2,1)S(1)} %collective-permute-done.21.a_ref, bf16[1024,128]{1,0:T(8,128)(2,1)S(1)} %collective-permute-done.22.b_ref, ...), custom_call_target="tpu_custom_call" | custom-call | tf_op jit(solution)/shard_map/finish/pallas_call | solution.py:299
  79.2 2.2 %collective-permute-done.18.a_ref = bf16[1024,128]{1,0:T(8,128)(2,1)S(1)} collective-permute-done((bf16[1024,128]{1,0:T(8,128)(2,1)S(1)}, bf16[1024,128]{1,0:T(8,128)(2,1)S(1)}, u32[]{:S(2)}, u32[]{:S(2)}) %collective-permute-start.18) | collective-permute-done | bytes 262176 | tf_op jit(solution)/shard_map/ppermute | solution.py:29
  81.4 5.6 %collective-permute-done.19.b_ref = bf16[1024,128]{1,0:T(8,128)(2,1)S(1)} collective-permute-done((bf16[1024,128]{1,0:T(8,128)(2,1)S(1)}, bf16[1024,128]{1,0:T(8,128)(2,1)S(1)}, u32[]{:S(2)}, u32[]{:S(2)}) %collective-permute-start.19) | collective-permute-done | bytes 262176 | tf_op jit(solution)/shard_map/ppermute | solution.py:29
  87.0 1.4 %collective-permute-done.20.c_ref = bf16[1024,128]{1,0:T(8,128)(2,1)S(1)} collective-permute-done((bf16[1024,128]{1,0:T(8,128)(2,1)S(1)}, bf16[1024,128]{1,0:T(8,128)(2,1)S(1)}, u32[]{:S(2)}, u32[]{:S(2)}) %collective-permute-start.20) | collective-permute-done | bytes 262176 | tf_op jit(solution)/shard_map/ppermute | solution.py:29
  88.4 1.0 %finish.3 = f32[256,1024]{1,0:T(8,128)} custom-call(f32[2,1024,128]{2,1,0:T(8,128)S(1)} %get-tuple-element.24.sq_ref, f32[1024,128]{1,0:T(8,128)S(1)} %get-tuple-element.31.own_ref, bf16[1024,128]{1,0:T(8,128)(2,1)S(1)} %collective-permute-done.18.a_ref, bf16[1024,128]{1,0:T(8,128)(2,1)S(1)} %collective-permute-done.19.b_ref, ...), custom_call_target="tpu_custom_call", output_to_operand_aliasing={{}: (5, {})} | custom-call | tf_op jit(solution)/shard_map/finish/pallas_call | solution.py:299
  (14 shorter events, 0.0 us)
Async XLA Ops:
  2.3 9.1 %copy-start = (bf16[2,528,128]{2,1,0:T(8,128)(2,1)S(1)}, bf16[2,528,128]{2,1,0:T(8,128)(2,1)}, u32[]{:S(2)}) copy-start(bf16[2,528,128]{2,1,0:T(8,128)(2,1)} %get-tuple-element.22.refs_0_) | copy-start | bytes 811012
  2.3 16.9 %collective-permute-start = (bf16[2,528,128]{2,1,0:T(8,128)(2,1)}, bf16[2,528,128]{2,1,0:T(8,128)(2,1)S(1)}, u32[]{:S(2)}, u32[]{:S(2)}) collective-permute-start(bf16[2,528,128]{2,1,0:T(8,128)(2,1)} %get-tuple-element.22.refs_0_), channel_id=1, source_target_pairs={{0,32},{1,33},{2,34},{3,35},{4,36},{5,37},{6,38},{7,39},{8,40},{9,... | collective-permute-start | bytes 811016 | tf_op jit(solution)/shard_map/ppermute | solution.py:29
  4.4 26.5 %all-to-all-start = ((bf16[16,144,128]{2,1,0:T(8,128)(2,1)}), bf16[16,144,128]{2,1,0:T(8,128)(2,1)S(1)}, u32[]{:S(2)}, u32[]{:S(2)}) async-start(bf16[16,144,128]{2,1,0:T(8,128)(2,1)} %get-tuple-element.23), calls=%async_computation | async-start | bytes 1179648 | tf_op jit(solution)/shard_map/all_to_all | solution.py:317
  11.5 14.7 %collective-permute-start.1 = (bf16[2,528,128]{2,1,0:T(8,128)(2,1)S(1)}, bf16[2,528,128]{2,1,0:T(8,128)(2,1)S(1)}, u32[]{:S(2)}, u32[]{:S(2)}) collective-permute-start(bf16[2,528,128]{2,1,0:T(8,128)(2,1)S(1)} %copy-done), channel_id=1, source_target_pairs={{0,96},{1,97},{2,98},{3,99},{4,100},{5,101},{6,102},{7,103},{8,104... | collective-permute-start | bytes 811016 | tf_op jit(solution)/shard_map/ppermute | solution.py:29
  14.1 12.1 %collective-permute-start.2 = (bf16[2,528,128]{2,1,0:T(8,128)(2,1)S(1)}, bf16[2,528,128]{2,1,0:T(8,128)(2,1)S(1)}, u32[]{:S(2)}, u32[]{:S(2)}) collective-permute-start(bf16[2,528,128]{2,1,0:T(8,128)(2,1)S(1)} %copy-done), channel_id=1, source_target_pairs={{0,64},{1,65},{2,66},{3,67},{4,68},{5,69},{6,70},{7,71},{8,72},{9,... | collective-permute-start | bytes 811016 | tf_op jit(solution)/shard_map/ppermute | solution.py:29
  15.2 11.5 %collective-permute-start.7 = (bf16[2,528,128]{2,1,0:T(8,128)(2,1)S(1)}, bf16[2,528,128]{2,1,0:T(8,128)(2,1)S(1)}, u32[]{:S(2)}, u32[]{:S(2)}) collective-permute-start(bf16[2,528,128]{2,1,0:T(8,128)(2,1)S(1)} %copy-done), channel_id=1, source_target_pairs={{0,0},{1,1},{2,16},{3,17},{4,32},{5,33},{6,48},{7,49},{8,8},{9,9},... | collective-permute-start | bytes 811016 | tf_op jit(solution)/shard_map/ppermute | solution.py:29
  15.9 11.4 %collective-permute-start.3 = (bf16[2,528,128]{2,1,0:T(8,128)(2,1)S(1)}, bf16[2,528,128]{2,1,0:T(8,128)(2,1)S(1)}, u32[]{:S(2)}, u32[]{:S(2)}) collective-permute-start(bf16[2,528,128]{2,1,0:T(8,128)(2,1)S(1)} %copy-done), channel_id=1, source_target_pairs={{0,16},{1,17},{2,18},{3,19},{4,20},{5,21},{6,22},{7,23},{8,24},{9,... | collective-permute-start | bytes 811016 | tf_op jit(solution)/shard_map/ppermute | solution.py:29
  19.2 10.4 %collective-permute-start.4 = (bf16[2,528,128]{2,1,0:T(8,128)(2,1)S(1)}, bf16[2,528,128]{2,1,0:T(8,128)(2,1)S(1)}, u32[]{:S(2)}, u32[]{:S(2)}) collective-permute-start(bf16[2,528,128]{2,1,0:T(8,128)(2,1)S(1)} %collective-permute-done.refs_1_), channel_id=1, source_target_pairs={{0,16},{1,17},{2,18},{3,19},{4,20},{5,21},{6,22},{7,23},{8,24},{9,... | collective-permute-start | bytes 811016 | tf_op jit(solution)/shard_map/ppermute | solution.py:29
  26.2 4.7 %collective-permute-start.5 = (bf16[2,528,128]{2,1,0:T(8,128)(2,1)S(1)}, bf16[2,528,128]{2,1,0:T(8,128)(2,1)S(1)}, u32[]{:S(2)}, u32[]{:S(2)}) collective-permute-start(bf16[2,528,128]{2,1,0:T(8,128)(2,1)S(1)} %collective-permute-done.1.refs_2_), channel_id=1, source_target_pairs={{0,16},{1,17},{2,18},{3,19},{4,20},{5,21},{6,22},{7,23},{8,24},{9,... | collective-permute-start | bytes 811016 | tf_op jit(solution)/shard_map/ppermute | solution.py:29
  26.2 4.7 %collective-permute-start.6 = (bf16[2,528,128]{2,1,0:T(8,128)(2,1)S(1)}, bf16[2,528,128]{2,1,0:T(8,128)(2,1)S(1)}, u32[]{:S(2)}, u32[]{:S(2)}) collective-permute-start(bf16[2,528,128]{2,1,0:T(8,128)(2,1)S(1)} %collective-permute-done.2.refs_3_), channel_id=1, source_target_pairs={{0,16},{1,17},{2,18},{3,19},{4,20},{5,21},{6,22},{7,23},{8,24},{9,... | collective-permute-start | bytes 811016 | tf_op jit(solution)/shard_map/ppermute | solution.py:29
  26.7 11.4 %collective-permute-start.8 = (bf16[2,528,128]{2,1,0:T(8,128)(2,1)S(1)}, bf16[2,528,128]{2,1,0:T(8,128)(2,1)S(1)}, u32[]{:S(2)}, u32[]{:S(2)}) collective-permute-start(bf16[2,528,128]{2,1,0:T(8,128)(2,1)S(1)} %collective-permute-done.7), channel_id=1, source_target_pairs={{0,32},{1,33},{2,34},{3,35},{4,36},{5,37},{6,38},{7,39},{8,40},{9,... | collective-permute-start | bytes 811016 | tf_op jit(solution)/shard_map/ppermute | solution.py:29
  27.3 14.5 %collective-permute-start.9 = (bf16[2,528,128]{2,1,0:T(8,128)(2,1)S(1)}, bf16[2,528,128]{2,1,0:T(8,128)(2,1)}, u32[]{:S(2)}, u32[]{:S(2)}) collective-permute-start(bf16[2,528,128]{2,1,0:T(8,128)(2,1)S(1)} %collective-permute-done.7), channel_id=1, source_target_pairs={{0,96},{1,97},{2,98},{3,99},{4,100},{5,101},{6,102},{7,103},{8,104... | collective-permute-start | bytes 811016 | tf_op jit(solution)/shard_map/ppermute | solution.py:29
  29.7 13.7 %collective-permute-start.10 = (bf16[2,528,128]{2,1,0:T(8,128)(2,1)S(1)}, bf16[2,528,128]{2,1,0:T(8,128)(2,1)}, u32[]{:S(2)}, u32[]{:S(2)}) collective-permute-start(bf16[2,528,128]{2,1,0:T(8,128)(2,1)S(1)} %collective-permute-done.7), channel_id=1, source_target_pairs={{0,64},{1,65},{2,66},{3,67},{4,68},{5,69},{6,70},{7,71},{8,72},{9,... | collective-permute-start | bytes 811016 | tf_op jit(solution)/shard_map/ppermute | solution.py:29
  34.4 10.1 %collective-permute-start.11 = (bf16[1024,128]{1,0:T(8,128)(2,1)S(1)}, bf16[1024,128]{1,0:T(8,128)(2,1)S(1)}, u32[]{:S(2)}, u32[]{:S(2)}) collective-permute-start(bf16[1024,128]{1,0:T(8,128)(2,1)S(1)} %get-tuple-element.25.refs_0_), channel_id=1, source_target_pairs={{0,8},{1,9},{2,10},{3,11},{4,12},{5,13},{6,14},{7,15},{8,0},{9,1},... | collective-permute-start | bytes 786440 | tf_op jit(solution)/shard_map/ppermute | solution.py:29
  36.1 15.5 %collective-permute-start.12 = (bf16[1024,128]{1,0:T(8,128)(2,1)S(1)}, bf16[1024,128]{1,0:T(8,128)(2,1)S(1)}, u32[]{:S(2)}, u32[]{:S(2)}) collective-permute-start(bf16[1024,128]{1,0:T(8,128)(2,1)S(1)} %get-tuple-element.25.refs_0_), channel_id=1, source_target_pairs={{0,9},{1,8},{2,11},{3,10},{4,13},{5,12},{6,15},{7,14},{8,1},{9,0},... | collective-permute-start | bytes 786440 | tf_op jit(solution)/shard_map/ppermute | solution.py:29
  38.1 13.5 %collective-permute-start.13 = (bf16[1024,128]{1,0:T(8,128)(2,1)S(1)}, bf16[1024,128]{1,0:T(8,128)(2,1)S(1)}, u32[]{:S(2)}, u32[]{:S(2)}) collective-permute-start(bf16[1024,128]{1,0:T(8,128)(2,1)S(1)} %get-tuple-element.25.refs_0_), channel_id=1, source_target_pairs={{0,1},{1,0},{2,3},{3,2},{4,5},{5,4},{6,7},{7,6},{8,9},{9,8},{10,11... | collective-permute-start | bytes 786440 | tf_op jit(solution)/shard_map/ppermute | solution.py:29
  51.6 4.8 %collective-permute-start.14 = (bf16[4,2,528,128]{3,2,1,0:T(8,128)(2,1)S(1)}, bf16[4,2,528,128]{3,2,1,0:T(8,128)(2,1)S(1)}, u32[]{:S(2)}, u32[]{:S(2)}) collective-permute-start(bf16[4,2,528,128]{3,2,1,0:T(8,128)(2,1)S(1)} %pad_maximum_fusion.part.same), channel_id=1, source_target_pairs={{0,16},{1,17},{2,18},{3,19},{4,20},{5,21},{6,22},{7,23},{8,24},{9,... | collective-permute-start | bytes 3244040 | tf_op jit(solution)/shard_map/ppermute | solution.py:29
  51.6 13.4 %collective-permute-start.17 = (bf16[1024,128]{1,0:T(8,128)(2,1)S(1)}, bf16[1024,128]{1,0:T(8,128)(2,1)S(1)}, u32[]{:S(2)}, u32[]{:S(2)}) collective-permute-start(bf16[1024,128]{1,0:T(8,128)(2,1)S(1)} %get-tuple-element.30.refs_0_), channel_id=1, source_target_pairs={{0,1},{1,0},{2,3},{3,2},{4,5},{5,4},{6,7},{7,6},{8,9},{9,8},{10,11... | collective-permute-start | bytes 786440 | tf_op jit(solution)/shard_map/ppermute | solution.py:29
  52.9 14.5 %collective-permute-start.16 = (bf16[1024,128]{1,0:T(8,128)(2,1)S(1)}, bf16[1024,128]{1,0:T(8,128)(2,1)S(1)}, u32[]{:S(2)}, u32[]{:S(2)}) collective-permute-start(bf16[1024,128]{1,0:T(8,128)(2,1)S(1)} %get-tuple-element.30.refs_0_), channel_id=1, source_target_pairs={{0,9},{1,8},{2,11},{3,10},{4,13},{5,12},{6,15},{7,14},{8,1},{9,0},... | collective-permute-start | bytes 786440 | tf_op jit(solution)/shard_map/ppermute | solution.py:29
  54.0 13.4 %collective-permute-start.15 = (bf16[1024,128]{1,0:T(8,128)(2,1)S(1)}, bf16[1024,128]{1,0:T(8,128)(2,1)S(1)}, u32[]{:S(2)}, u32[]{:S(2)}) collective-permute-start(bf16[1024,128]{1,0:T(8,128)(2,1)S(1)} %get-tuple-element.30.refs_0_), channel_id=1, source_target_pairs={{0,8},{1,9},{2,10},{3,11},{4,12},{5,13},{6,14},{7,15},{8,0},{9,1},... | collective-permute-start | bytes 786440 | tf_op jit(solution)/shard_map/ppermute | solution.py:29
  61.1 13.7 %collective-permute-start.21 = (bf16[1024,128]{1,0:T(8,128)(2,1)S(1)}, bf16[1024,128]{1,0:T(8,128)(2,1)S(1)}, u32[]{:S(2)}, u32[]{:S(2)}) collective-permute-start(bf16[1024,128]{1,0:T(8,128)(2,1)S(1)} %get-tuple-element.36), channel_id=1, source_target_pairs={{0,2},{1,3},{2,0},{3,1},{4,6},{5,7},{6,4},{7,5},{8,10},{9,11},{10,... | collective-permute-start | bytes 786440 | tf_op jit(solution)/shard_map/ppermute | solution.py:29
  61.8 14.9 %collective-permute-start.22 = (bf16[1024,128]{1,0:T(8,128)(2,1)S(1)}, bf16[1024,128]{1,0:T(8,128)(2,1)S(1)}, u32[]{:S(2)}, u32[]{:S(2)}) collective-permute-start(bf16[1024,128]{1,0:T(8,128)(2,1)S(1)} %get-tuple-element.37), channel_id=1, source_target_pairs={{0,6},{1,7},{2,4},{3,5},{4,2},{5,3},{6,0},{7,1},{8,14},{9,15},{10,... | collective-permute-start | bytes 786440 | tf_op jit(solution)/shard_map/ppermute | solution.py:29
  65.0 13.1 %collective-permute-start.23 = (bf16[1024,128]{1,0:T(8,128)(2,1)S(1)}, bf16[1024,128]{1,0:T(8,128)(2,1)S(1)}, u32[]{:S(2)}, u32[]{:S(2)}) collective-permute-start(bf16[1024,128]{1,0:T(8,128)(2,1)S(1)} %get-tuple-element.38), channel_id=1, source_target_pairs={{0,4},{1,5},{2,6},{3,7},{4,0},{5,1},{6,2},{7,3},{8,12},{9,13},{10,... | collective-permute-start | bytes 786440 | tf_op jit(solution)/shard_map/ppermute | solution.py:29
  70.9 10.5 %collective-permute-start.18 = (bf16[1024,128]{1,0:T(8,128)(2,1)S(1)}, bf16[1024,128]{1,0:T(8,128)(2,1)S(1)}, u32[]{:S(2)}, u32[]{:S(2)}) collective-permute-start(bf16[1024,128]{1,0:T(8,128)(2,1)S(1)} %get-tuple-element.32), channel_id=1, source_target_pairs={{0,2},{1,3},{2,0},{3,1},{4,6},{5,7},{6,4},{7,5},{8,10},{9,11},{10,... | collective-permute-start | bytes 786440 | tf_op jit(solution)/shard_map/ppermute | solution.py:29
  71.6 15.4 %collective-permute-start.19 = (bf16[1024,128]{1,0:T(8,128)(2,1)S(1)}, bf16[1024,128]{1,0:T(8,128)(2,1)S(1)}, u32[]{:S(2)}, u32[]{:S(2)}) collective-permute-start(bf16[1024,128]{1,0:T(8,128)(2,1)S(1)} %get-tuple-element.33), channel_id=1, source_target_pairs={{0,6},{1,7},{2,4},{3,5},{4,2},{5,3},{6,0},{7,1},{8,14},{9,15},{10,... | collective-permute-start | bytes 786440 | tf_op jit(solution)/shard_map/ppermute | solution.py:29
  74.8 13.5 %collective-permute-start.20 = (bf16[1024,128]{1,0:T(8,128)(2,1)S(1)}, bf16[1024,128]{1,0:T(8,128)(2,1)S(1)}, u32[]{:S(2)}, u32[]{:S(2)}) collective-permute-start(bf16[1024,128]{1,0:T(8,128)(2,1)S(1)} %get-tuple-element.34), channel_id=1, source_target_pairs={{0,4},{1,5},{2,6},{3,7},{4,0},{5,1},{6,2},{7,3},{8,12},{9,13},{10,... | collective-permute-start | bytes 786440 | tf_op jit(solution)/shard_map/ppermute | solution.py:29
